TPU v7x, 1024 devices: a whole 4x4x32 slice. The times are simulated.
1024 devices in a mesh: table: 64 (over z, core), cuts: 16 (over x, y).
Axes of the slice: x: 4, y: 4, z: 32, core: 2. Of those that a mesh axis runs over, the one named last changes fastest.
Arguments:
- embedding: bfloat16 [1048576, 128], P('table', 'cuts'), may hold values from -6 to 6
- cross_weight: bfloat16 [4096, 4096], P(None, 'cuts'), may hold values from -0.09375 to 0.09375
- cross_bias: float32 [4096], P('cuts'), may hold values from -5 to 5
- upstream: bfloat16 [8192, 4096], P('table', 'cuts'), may hold values from -6 to 6
- unique_rows: int32 [64, 64, 16], P(None, 'table'), may hold values from 0 to 16383, as said below
- lookup_slot: int32 [64, 8192], P('table'), may hold values from 0 to 1023, as said below
- bag_of_lookup: int32 [64, 8192], P('table'), may hold values from 0 to 4095, never falling along the last dimension, each value on 1 to 8 neighbouring positions
Outputs:
- cross_out: bfloat16 [8192, 4096], P('table', 'cuts')
- row_grads: float32 [1048576, 128], P('table', 'cuts')
Inputs may be any that keep to these rules, and one draw needn't show every extreme that they name: For each s and p the 16 entries unique_rows[s, p, :] are distinct local rows of owner p. lookup_slot[s, l] = p * 16 + j names slot j of shard s's request list to owner p.
All inputs are finite; a program needn't handle non-finite values.
Results may differ from a plain program's by a relative error of at most 0.0095.
Values may be sent and summed in bfloat16 or wider, within the bound.
No kernel may reach another device: no remote copies, remote signals or barrier semaphores. Data moves between devices by JAX's collectives and lax.ppermute only.
A program may use at most 64 MiB of HBM per device.

v0:
```python
import math

import jax
import jax.numpy as jnp
from jax import lax
from jax.sharding import PartitionSpec as P


def pool_sorted(looked, bag_index, bag_count):
    total, width_cols = looked.shape
    block = math.gcd(total, 512)
    steps = total // block
    looked_blocks = looked.reshape(steps, block, width_cols)
    bag_blocks = bag_index.reshape(steps, block)
    offsets = jnp.arange(block, dtype=jnp.int32)

    def pool_add_block(acc, item):
        rows, bags = item
        first = bags[0]
        indicator = (bags[:, None] - first == offsets[None, :]).astype(jnp.bfloat16)
        part_sum = lax.dot_general(
            indicator, rows, (((0,), (0,)), ((), ())), preferred_element_type=jnp.float32
        )
        window = lax.dynamic_slice_in_dim(acc, first, block, 0)
        return (lax.dynamic_update_slice_in_dim(acc, window + part_sum, first, 0), None)

    start = jnp.zeros((bag_count + block, width_cols), jnp.float32)
    summed, unused = lax.scan(pool_add_block, start, (looked_blocks, bag_blocks))
    return summed[:bag_count]


def split_exact(values):
    upper = values.astype(jnp.bfloat16)
    rest = values - lax.optimization_barrier(upper).astype(jnp.float32)
    middle = rest.astype(jnp.bfloat16)
    lower = (rest - lax.optimization_barrier(middle).astype(jnp.float32)).astype(jnp.bfloat16)
    return jnp.concatenate([upper, middle, lower], axis=1)


def spread_slots(values, slot_index, slot_count):
    total, width_cols = values.shape
    block = math.gcd(total, 512)
    steps = total // block
    pieces = split_exact(values).reshape(steps, block, 3 * width_cols)
    slot_blocks = slot_index.reshape(steps, block)
    targets = jnp.arange(slot_count, dtype=jnp.int32)

    def spread_add_block(acc, item):
        rows, slots = item
        indicator = (slots[:, None] == targets[None, :]).astype(jnp.bfloat16)
        return (
            acc
            + lax.dot_general(
                indicator, rows, (((0,), (0,)), ((), ())), preferred_element_type=jnp.float32
            ),
            None,
        )

    start = jnp.zeros((slot_count, 3 * width_cols), jnp.float32)
    summed, unused = lax.scan(spread_add_block, start, (pieces, slot_blocks))
    return (
        summed[:, :width_cols]
        + summed[:, width_cols : 2 * width_cols]
        + summed[:, 2 * width_cols :]
    )


def per_device(
    embedding, cross_weight, cross_bias, upstream, unique_rows, lookup_slot, bag_of_lookup
):
    owners = lax.axis_size("table")
    rows_dev, columns = embedding.shape
    capacity = unique_rows.shape[2]
    batch, share = upstream.shape
    tables = share // columns
    bag_count = batch * tables
    slot_count = owners * capacity
    row_ids = unique_rows.reshape(slot_count)
    picked = jnp.take(embedding, row_ids, axis=0).reshape(owners, 1, capacity, columns)
    arrived = lax.all_to_all(picked, "table", split_axis=0, concat_axis=1, tiled=True).reshape(
        slot_count, columns
    )
    slot_index = lookup_slot.reshape(-1)
    bag_index = bag_of_lookup.reshape(-1)
    looked = jnp.take(arrived, slot_index, axis=0)
    pooled = pool_sorted(looked, bag_index, bag_count).astype(jnp.bfloat16)
    local_base = pooled.reshape(batch, share)
    weight_rows = cross_weight
    mix = (
        jnp.dot(
            lax.all_gather(local_base, "cuts", axis=1, tiled=True),
            weight_rows,
            preferred_element_type=jnp.float32,
        )
        + cross_bias
    )
    base_wide = local_base.astype(jnp.float32)
    cross_out = (base_wide * mix + base_wide).astype(jnp.bfloat16)
    grad_wide = upstream.astype(jnp.float32)
    mix_grad = (grad_wide * base_wide).astype(jnp.bfloat16)
    local_term = grad_wide * (mix + 1.0)
    weight_rows = cross_weight
    spread = lax.psum_scatter(
        lax.dot_general(
            weight_rows, mix_grad, (((1,), (1,)), ((), ())), preferred_element_type=jnp.float32
        ).astype(jnp.bfloat16),
        "cuts",
        scatter_dimension=0,
        tiled=True,
    ).astype(jnp.float32)
    base_grad = local_term + spread.T
    per_lookup = jnp.take(base_grad.reshape(bag_count, columns), bag_index, axis=0)
    slot_grad = spread_slots(per_lookup, slot_index, slot_count)
    returned = lax.all_to_all(
        slot_grad.reshape(1, owners, capacity, columns),
        "table",
        split_axis=1,
        concat_axis=0,
        tiled=True,
    )
    row_grads = jax.ops.segment_sum(
        returned.reshape(slot_count, columns), row_ids, num_segments=rows_dev
    )
    return (cross_out, row_grads)


def solution(mesh):
    return jax.shard_map(
        per_device,
        mesh=mesh,
        in_specs=(
            P("table", "cuts"),
            P(None, "cuts"),
            P("cuts"),
            P("table", "cuts"),
            P(None, "table", None),
            P("table", None),
            P("table", None),
        ),
        out_specs=(P("table", "cuts"), P("table", "cuts")),
        check_vma=False,
    )
```

profile of v0, /device:TPU:1, one launch (start us, length us, event | category | flops | bytes accessed | tf_op | source)
XLA Modules:
  0.0 469.2 jit_solution(7841127174586267381)
XLA Ops:
  7.2 0.9 compare_and_fusion.2
  8.0 0.8 copy.41
  9.0 4.0 copy.42
  13.0 5.6 %gather_fusion = bf16[1024,8]{1,0:T(8,128)(2,1)S(1)} fusion(bf16[16384,8]{1,0:T(8,128)(2,1)} %copy.42, s32[1024]{0:T(1024)S(1)} %broadcast_clamp_fusion.2), kind=kCustom, calls=%fused_computation | custom fusion | bytes 36864 | tf_op jit(solution)/shard_map/jit(_take)/gather | solution.py:79
  18.8 0.7 broadcast_select_fusion
  19.5 30.4 %all-to-all-start = ((bf16[64,1,16,8]{2,3,1,0:T(8,128)(2,1)}), bf16[64,1,16,8]{2,3,1,0:T(8,128)(2,1)S(1)}, u32[]{:S(2)}, u32[]{:S(2)}) async-start(bf16[64,1,16,8]{2,3,1,0:T(8,128)(2,1)} %broadcast_select_fusion), calls=%async_computation | async-start | bytes 262144 | tf_op jit(solution)/shard_map/all_to_all | solution.py:80
  50.6 0.7 reduce.7
  51.3 0.7 reduce.6
  52.0 28.6 %all-to-all-done = bf16[64,1,16,8]{2,3,1,0:T(8,128)(2,1)S(1)} async-done(((bf16[64,1,16,8]{2,3,1,0:T(8,128)(2,1)}), bf16[64,1,16,8]{2,3,1,0:T(8,128)(2,1)S(1)}, u32[]{:S(2)}, u32[]{:S(2)}) %all-to-all-start) | async-done | bytes 16416 | tf_op jit(solution)/shard_map/all_to_all | solution.py:80
  80.8 29.4 %gather_fusion.1 = bf16[8192,8]{1,0:T(8,128)(2,1)} fusion(bf16[1024,8]{1,0:T(8,128)(2,1)S(1)} %bitcast.56, s32[8192]{0:T(1024)S(1)} %broadcast_clamp_fusion.1), kind=kCustom, calls=%fused_computation.1 | custom fusion | bytes 294912 | tf_op jit(solution)/shard_map/jit(_take)/gather | solution.py:85
  110.2 1.8 copy.45
  112.1 61.9 %while.22 = (s32[]{:T(128)}, f32[4608,8]{0,1:T(8,128)S(1)}, s32[16,512]{1,0:T(8,128)S(1)}, bf16[16,512,8]{1,2,0:T(8,128)(2,1)S(1)}, s32[]{:T(128)}, /*index=5*/s32[]{:T(128)}, s32[]{:T(128)}) while((s32[]{:T(128)}, f32[4608,8]{0,1:T(8,128)S(1)}, s32[16,512]{1,0:T(8,128)S(1)}, bf16[16,512,8]{1,2,0:T(8,128)(2,1)S(1)}, s32[]{:T(128)}, ...), condition=%wide.region_1.2_spmd.clone, body=%wide.region_0.1_spmd.clone.sunk | while | flops 4461061 | bytes 80023 | solution.py:28
  114.6 0.7 dynamic-slice_subtract_fusion.2
  118.3 0.7 dynamic-slice_subtract_fusion.2
  122.1 0.7 dynamic-slice_subtract_fusion.2
  129.9 0.7 dynamic-slice_subtract_fusion.2
  149.3 0.7 dynamic-slice_subtract_fusion.2
  174.5 2.1 reshape.194
  176.7 2.7 fusion.14
  179.4 57.4 %all-gather.2.cloned.1.call-done = bf16[128,4096]{1,0:T(8,128)(2,1)} async-done(((bf16[128,256]{1,0:T(8,128)(2,1)}), bf16[128,4096]{1,0:T(8,128)(2,1)}) %all-gather.2.cloned.1.call-update) | async-done | bytes 1048592 | tf_op jit(solution)/shard_map/all_gather | solution.py:91
  236.9 113.4 %reduce-scatter.2.cloned.1.call-done = bf16[256,128]{0,1:T(8,128)(2,1)} async-done(((bf16[4096,128]{0,1:T(8,128)(2,1)}), bf16[256,128]{0,1:T(8,128)(2,1)}) %reduce-scatter.2.cloned.1.call-update) | async-done | bytes 65552 | tf_op jit(solution)/shard_map/reduce_scatter | solution.py:103
  350.3 2.3 fusion.18
  352.6 2.5 reshape.196
  355.1 29.4 %gather_fusion.2 = f32[8192,8]{1,0:T(8,128)} fusion(f32[4096,8]{1,0:T(8,128)} %reshape.196, s32[8192]{0:T(1024)S(1)} %broadcast_clamp_fusion), kind=kCustom, calls=%fused_computation.2 | custom fusion | bytes 557056 | tf_op jit(solution)/shard_map/jit(_take)/gather | solution.py:112
  384.5 2.8 copy.48
  387.6 8.7 %while.23 = (s32[]{:T(128)}, f32[1024,24]{0,1:T(8,128)S(1)}, s32[16,512]{1,0:T(8,128)S(1)}, bf16[16,512,24]{1,2,0:T(8,128)(2,1)S(1)}, s32[]{:T(128)}, /*index=5*/s32[]{:T(128)}) while((s32[]{:T(128)}, f32[1024,24]{0,1:T(8,128)S(1)}, s32[16,512]{1,0:T(8,128)S(1)}, bf16[16,512,24]{1,2,0:T(8,128)(2,1)S(1)}, s32[]{:T(128)}, ...), condition=%wide.region_4.5_spmd.clone, body=%wide.region_3.4_spmd.clone.sunk | while | flops 25739268 | bytes 227423 | solution.py:60
  396.6 0.8 reshape.252
  397.4 25.4 %all-to-all-start.1 = ((f32[64,1,128]{2,1,0:T(1,128)}), f32[64,1,128]{2,1,0:T(1,128)S(1)}, u32[]{:S(2)}, u32[]{:S(2)}) async-start(f32[64,1,128]{2,1,0:T(1,128)} %reshape.252), calls=%async_computation.2 | async-start | bytes 65536 | tf_op jit(solution)/shard_map/all_to_all | solution.py:114
  422.9 22.3 %all-to-all-done.1 = f32[64,1,128]{2,1,0:T(1,128)S(1)} async-done(((f32[64,1,128]{2,1,0:T(1,128)}), f32[64,1,128]{2,1,0:T(1,128)S(1)}, u32[]{:S(2)}, u32[]{:S(2)}) %all-to-all-start.1) | async-done | bytes 32800 | tf_op jit(solution)/shard_map/all_to_all | solution.py:114
  445.7 0.7 reduce.8
  446.8 9.7 %scatter_custom_fusion = f32[16384,8]{1,0:T(8,128)} fusion(s32[1024]{0:T(1024)S(1)} %reshape.227, f32[1024,8]{1,0:T(8,128)S(1)} %bitcast.62, f32[]{:T(128)} %constant.54.clone.1), kind=kCustom, calls=%fused_computation.24 | custom fusion | flops 8192 | bytes 524292 | tf_op jit(solution)/shard_map/scatter-add | solution.py:121
  456.5 5.9 %copy.53 = f32[16384,8]{0,1:T(8,128)} copy(f32[16384,8]{1,0:T(8,128)} %scatter_custom_fusion) | data formatting | bytes 1048576
  (139 shorter events, 38.5 us)
Async XLA Ops:
  7.2 169.5 %copy-start = (bf16[4096,256]{1,0:T(8,128)(2,1)S(1)}, bf16[4096,256]{1,0:T(8,128)(2,1)}, u32[]{:S(2)}) copy-start(bf16[4096,256]{1,0:T(8,128)(2,1)} %param.12) | copy-start | bytes 6291460
  13.0 36.9 %copy-start.4 = (s32[1,8192]{1,0:T(1,128)S(1)}, s32[1,8192]{1,0:T(1,128)}, u32[]{:S(2)}) copy-start(s32[1,8192]{1,0:T(1,128)} %param.16) | copy-start | bytes 98308
  13.0 38.3 %copy-start.2 = (s32[1,8192]{1,0:T(1,128)S(1)}, s32[1,8192]{1,0:T(1,128)}, u32[]{:S(2)}) copy-start(s32[1,8192]{1,0:T(1,128)} %param.17) | copy-start | bytes 98308
  19.5 61.1 %all-to-all-start = ((bf16[64,1,16,8]{2,3,1,0:T(8,128)(2,1)}), bf16[64,1,16,8]{2,3,1,0:T(8,128)(2,1)S(1)}, u32[]{:S(2)}, u32[]{:S(2)}) async-start(bf16[64,1,16,8]{2,3,1,0:T(8,128)(2,1)} %broadcast_select_fusion), calls=%async_computation | async-start | bytes 262144 | tf_op jit(solution)/shard_map/all_to_all | solution.py:80
  49.9 186.9 %all-gather.2.cloned.1.call-start = ((), (), s32[]{:S(2)}) async-start(), calls=%async_computation.3 | async-start | bytes 1114112 | tf_op jit(solution)/shard_map/all_gather | solution.py:91
  112.1 64.5 %copy-start.3 = (bf16[128,256]{1,0:T(8,128)(2,1)S(1)}, bf16[128,256]{1,0:T(8,128)(2,1)}, u32[]{:S(2)}) copy-start(bf16[128,256]{1,0:T(8,128)(2,1)} %param.14) | copy-start | bytes 196612
  176.6 173.7 %copy-start.1 = (bf16[128,256]{1,0:T(8,128)(2,1)S(1)}, bf16[128,256]{1,0:T(8,128)(2,1)}, u32[]{:S(2)}) copy-start(bf16[128,256]{1,0:T(8,128)(2,1)} %reshape.194) | copy-start | bytes 196612
  176.6 173.7 %copy-start.5 = (f32[256]{0:T(256)S(1)}, f32[256]{0:T(256)}, u32[]{:S(2)}) copy-start(f32[256]{0:T(256)} %param.13) | copy-start | bytes 3076
  176.6 173.7 %reduce-scatter.2.cloned.1.call-start = ((), (), s32[]{:S(2)}) async-start(), calls=%async_computation.4 | async-start | bytes 1114112 | tf_op jit(solution)/shard_map/reduce_scatter | solution.py:103
  397.4 47.8 %all-to-all-start.1 = ((f32[64,1,128]{2,1,0:T(1,128)}), f32[64,1,128]{2,1,0:T(1,128)S(1)}, u32[]{:S(2)}, u32[]{:S(2)}) async-start(f32[64,1,128]{2,1,0:T(1,128)} %reshape.252), calls=%async_computation.2 | async-start | bytes 65536 | tf_op jit(solution)/shard_map/all_to_all | solution.py:114
Sparse Core Ops, SparseCore 0:
  176.7 60.1 all-gather.1
  242.1 108.1 reduce-scatter.1
where the time goes:
time: 470 us; the launch traced here: 469 us
  waiting for transfers between devices  222 us (47%)
  local copies, waits for them, and re-layouts  103 us (22%)
  starting transfers between devices  55.9 us (12%)
  loops' own time  32.1 us (7%)
  other arithmetic  24.3 us (5%)
  matrix products  17.7 us (4%)
  between operations  14.4 us (3%)
    reduce_scatter x1, waiting for transfers between devices, per_device(): lax.psum_scatter(lax.dot_general(weight_rows, mix_grad, (((1,), (1,)), ((...  113 us
    all_gather x1, waiting for transfers between devices, per_device(): lax.all_gather(local_base, 'cuts', axis=1, tiled=True)  57.4 us
    gather x2, local copies, waits for them, and re-layouts, per_device(): jnp.take(base_grad.reshape(bag_count, columns), bag_index, axis=0)  32.2 us
    another operation x1, loops' own time, pool_sorted(): lax.scan(pool_add_block, start, (looked_blocks, bag_blocks))  31.6 us
    gather x2, local copies, waits for them, and re-layouts, per_device(): looked = jnp.take(arrived, slot_index, axis=0)  31.2 us
    all_to_all x1, starting transfers between devices, per_device(): lax.all_to_all(picked, 'table', split_axis=0, concat_axis=1, tiled=True)  30.4 us
    all_to_all x1, waiting for transfers between devices, per_device(): lax.all_to_all(picked, 'table', split_axis=0, concat_axis=1, tiled=True)  28.6 us
    all_to_all x1, starting transfers between devices, per_device(): lax.all_to_all(slot_grad.reshape(1, owners, capacity, columns), 'table',...  25.4 us
  transfers between devices with their start and end apart: 4, of which 4 were waited for; matrix products, arithmetic and copies ran while one was open for 1% of the time, Pallas kernels for 0%

commit v1 on v0

v1 whole, which is shorter than its diff:
```python
import functools

import jax
import jax.numpy as jnp
from jax import lax
from jax.experimental import pallas as pl
from jax.experimental.pallas import tpu as pltpu
from jax.sharding import PartitionSpec as P

LANES = 128
LOOK_BLOCK = 256
WINDOW = LOOK_BLOCK + 8
NT = (((1,), (1,)), ((), ()))


def dot(a, b):
    return jnp.dot(a, b, preferred_element_type=jnp.float32)


def dot_nt(a, b):
    return lax.dot_general(a, b, NT, preferred_element_type=jnp.float32)


def swap_blocks(parts, width):
    parts = list(parts)
    count = len(parts)
    lanes = parts[0].shape[1]
    block = lax.broadcasted_iota(jnp.int32, parts[0].shape, 1) // width
    step = 1
    while step < count:
        high = (block & step) != 0
        for a in range(count):
            if a & step:
                continue
            low_part, high_part = parts[a], parts[a | step]
            parts[a] = jnp.where(high, pltpu.roll(high_part, step * width, 1), low_part)
            parts[a | step] = jnp.where(
                high, high_part, pltpu.roll(low_part, lanes - step * width, 1)
            )
        step *= 2
    return parts


def row_halves(ids_ref, group, per):
    ids = jnp.concatenate([ids_ref[group * per + k : group * per + k + 1, :] for k in range(per)], axis=1)
    return ids // LANES, ids % LANES


def pick_kernel(ids_ref, emb_ref, out_ref):
    cap, shards = ids_ref.shape
    columns = out_ref.shape[1] // cap
    highs = emb_ref.shape[0] // columns
    per = 256 // shards
    pieces = []
    for group in range(cap // per):
        hi, lo = row_halves(ids_ref, group, per)
        n = hi.shape[1]
        low_hot = (lax.broadcasted_iota(jnp.int32, (LANES, n), 0) == lo).astype(jnp.float32).astype(jnp.bfloat16)
        wide = dot(emb_ref[...], low_hot).reshape(highs, columns, n)
        high_hot = lax.broadcasted_iota(jnp.int32, (highs, columns, n), 0) == hi[None]
        found = jnp.sum(jnp.where(high_hot, wide, 0.0), axis=0)
        for k in range(per):
            pieces.append(found[:, k * shards : (k + 1) * shards])
    out_ref[...] = jnp.concatenate(pieces, axis=0).T.astype(out_ref.dtype)


def scatter_kernel(ids_ref, grad_ref, out_ref):
    cap, shards = ids_ref.shape
    columns = grad_ref.shape[1] // cap
    highs = out_ref.shape[0] // columns
    per = 256 // shards
    turned = grad_ref[...].astype(jnp.float32).T
    for group in range(cap // per):
        hi, lo = row_halves(ids_ref, group, per)
        n = hi.shape[1]
        low_hot = (lax.broadcasted_iota(jnp.int32, (LANES, n), 0) == lo).astype(jnp.float32).astype(jnp.bfloat16)
        values = jnp.concatenate(
            [turned[(group * per + k) * columns : (group * per + k + 1) * columns] for k in range(per)],
            axis=1,
        )
        high_hot = lax.broadcasted_iota(jnp.int32, (highs, columns, n), 0) == hi[None]
        spread = jnp.where(high_hot, values[None], 0.0).reshape(highs * columns, n).astype(jnp.bfloat16)
        part = dot_nt(spread, low_hot)
        if group == 0:
            out_ref[...] = part
        else:
            out_ref[...] += part


def count_kernel(cap, tables, firsts_ref, slot_ref, bag_ref, out_ref, acc):
    look = slot_ref.shape[1]
    slots = out_ref.shape[1]
    owners = slots // cap
    batch = out_ref.shape[0] // tables
    for n in range(slots // LANES):
        acc[n, 0:8, :] = jnp.zeros((8, LANES), jnp.float32)

    def body(i, carry):
        at = pl.ds(pl.multiple_of(i * LOOK_BLOCK, LOOK_BLOCK), LOOK_BLOCK)
        start = pl.multiple_of(firsts_ref[0, i * LOOK_BLOCK] // 8 * 8, 8)
        bags = bag_ref[:, at] - start
        slot = slot_ref[:, at]
        order = slot % cap * owners + slot // cap
        bag_hot = (lax.broadcasted_iota(jnp.int32, (WINDOW, LOOK_BLOCK), 0) == bags).astype(jnp.float32).astype(jnp.bfloat16)
        for n in range(slots // 256):
            slot_hot = (
                (lax.broadcasted_iota(jnp.int32, (256, LOOK_BLOCK), 0) + n * 256 == order)
                .astype(jnp.float32)
                .astype(jnp.bfloat16)
            )
            part = dot_nt(bag_hot, slot_hot)
            for m in range(2):
                cols = slice(m * LANES, (m + 1) * LANES)
                acc[2 * n + m, pl.ds(start, 8), :] += part[0:8, cols]
                acc[2 * n + m, pl.ds(start + 8, WINDOW - 8), :] = part[8:, cols]
        return carry

    lax.fori_loop(0, look // LOOK_BLOCK, body, 0)
    for f in range(tables):
        row = (f % 2 * (tables // 2) + f // 2) * batch
        for n in range(slots // LANES):
            cols = slice(n * LANES, (n + 1) * LANES)
            out_ref[row : row + batch, cols] = acc[n, pl.ds(f, batch, stride=tables), :].astype(jnp.bfloat16)


def cross_kernel(cap, own_ref, rows_ref, count_ref, weight_ref, bias_ref, up_ref, out_ref, grad_ref, base_s, turned_s):
    cuts, owners, lanes = rows_ref.shape
    columns = lanes // cap
    batch, share = up_ref.shape
    pairs = share // (2 * columns)
    own = own_ref[0]

    picked = swap_blocks([rows_ref[q].astype(jnp.float32) for q in range(cuts)], columns)
    rows = jnp.concatenate(picked, axis=0).astype(jnp.bfloat16)
    wide = 2 * lanes
    r = lax.broadcasted_iota(jnp.int32, (lanes, wide), 0)
    l = lax.broadcasted_iota(jnp.int32, (lanes, wide), 1)
    same = (l // (2 * columns) == r // columns) & (l % columns == r % columns)
    odd = (l // columns) % 2 == 1
    put_even = jnp.where(same & ~odd, 1.0, 0.0).astype(jnp.bfloat16)
    put_odd = jnp.where(same & odd, 1.0, 0.0).astype(jnp.bfloat16)
    rows_even = dot(rows, put_even).astype(jnp.bfloat16)
    rows_odd = dot(rows, put_odd).astype(jnp.bfloat16)

    half = pairs * batch
    chunk = 4 * batch
    for c in range(half // chunk):
        at = c * chunk
        both = dot(count_ref[at : at + chunk, :], rows_even) + dot(
            count_ref[half + at : half + at + chunk, :], rows_odd
        )
        base_s[at : at + chunk, :] = both.astype(jnp.bfloat16)

    lane_block = lax.broadcasted_iota(jnp.int32, (batch, lanes), 1) // (2 * columns)
    per_half = lanes // (2 * columns)
    mix = jnp.zeros((batch, share), jnp.float32)
    own_base = [jnp.zeros((batch, lanes), jnp.float32) for _ in range(2)]
    weights = []
    for pair in range(pairs):
        base = base_s[pair * batch : (pair + 1) * batch, :]
        weight = jnp.concatenate(
            [
                weight_ref[q * share + pair * 2 * columns : q * share + (pair + 1) * 2 * columns, :]
                for q in range(cuts)
            ],
            axis=0,
        )
        mix = mix + dot(base, weight)
        mine = jnp.where(own < cuts // 2, base[:, :lanes].astype(jnp.float32), base[:, lanes:].astype(jnp.float32))
        shift = (pair % per_half - own % per_half + per_half) % per_half * (2 * columns)
        moved = pltpu.roll(mine, shift, 1)
        side = pair // per_half
        own_base[side] = jnp.where(lane_block == pair % per_half, moved, own_base[side])
    base_wide = jnp.concatenate(own_base, axis=1)
    mix = mix + bias_ref[...]
    out_ref[...] = (base_wide * mix + base_wide).astype(jnp.bfloat16)
    up = up_ref[...].astype(jnp.float32)
    mix_grad = (up * base_wide).astype(jnp.bfloat16)
    local = (up * (mix + 1.0)).T

    q_index = lax.broadcasted_iota(jnp.int32, (cuts, 2 * columns, batch), 0)
    for pair in range(pairs):
        weight = jnp.concatenate(
            [
                weight_ref[q * share + pair * 2 * columns : q * share + (pair + 1) * 2 * columns, :]
                for q in range(cuts)
            ],
            axis=0,
        )
        back = dot_nt(weight, mix_grad).reshape(cuts, 2 * columns, batch)
        term = local[pair * 2 * columns : (pair + 1) * 2 * columns]
        back = back + jnp.where(q_index == own, term[None], 0.0)
        at = pair * batch
        turned_s[:, at : at + batch] = back[:, :columns].reshape(lanes, batch).astype(jnp.bfloat16)
        turned_s[:, half + at : half + at + batch] = back[:, columns:].reshape(lanes, batch).astype(jnp.bfloat16)
    slot_grad = dot(turned_s[...], count_ref[...]).T
    parts = swap_blocks([slot_grad[j * owners : (j + 1) * owners] for j in range(cap)], columns)
    for q in range(cuts):
        grad_ref[q] = parts[q].astype(jnp.bfloat16)


def call(kernel, out_shape, in_spaces, scratch=(), limit=48, **kw):
    outs = jax.tree.map(lambda unused: pl.BlockSpec(memory_space=pltpu.VMEM), out_shape)
    return pl.pallas_call(
        kernel,
        out_shape=out_shape,
        in_specs=[pl.BlockSpec(memory_space=space) for space in in_spaces],
        out_specs=outs,
        scratch_shapes=list(scratch),
        compiler_params=pltpu.CompilerParams(vmem_limit_bytes=limit * 2**20),
        **kw,
    )


def pick(ids, emb, shards, lanes, **kw):
    V = pltpu.VMEM
    return call(pick_kernel, jax.ShapeDtypeStruct((shards, lanes), jnp.bfloat16), [V, V], **kw)(ids, emb)


def scatter(ids, grads, rows_out, **kw):
    V = pltpu.VMEM
    return call(scatter_kernel, jax.ShapeDtypeStruct((rows_out, LANES), jnp.float32), [V, V], **kw)(ids, grads)


def count(slot, bag, cap, tables, bags, slots, **kw):
    V, S = pltpu.VMEM, pltpu.SMEM
    return call(
        functools.partial(count_kernel, cap, tables),
        jax.ShapeDtypeStruct((bags, slots), jnp.bfloat16),
        [S, V, V],
        [pltpu.VMEM((slots // LANES, bags + WINDOW, LANES), jnp.float32)],
        **kw,
    )(bag, slot, bag)


def cross(own, rows, counts, weight, bias, up, cap, **kw):
    V, S = pltpu.VMEM, pltpu.SMEM
    cuts, owners, lanes = rows.shape
    batch, share = up.shape
    return call(
        functools.partial(cross_kernel, cap),
        (jax.ShapeDtypeStruct(up.shape, jnp.bfloat16), jax.ShapeDtypeStruct(rows.shape, jnp.bfloat16)),
        [S, V, V, V, V, V],
        [
            pltpu.VMEM((counts.shape[0] // 2, 2 * lanes), jnp.bfloat16),
            pltpu.VMEM((lanes, counts.shape[0]), jnp.bfloat16),
        ],
        **kw,
    )(own, rows, counts, weight, bias, up)


def per_device(embedding, cross_weight, cross_bias, upstream, unique_rows, lookup_slot, bag_of_lookup):
    owners = lax.axis_size("table")
    cuts = lax.axis_size("cuts")
    rows_dev, columns = embedding.shape
    cap = unique_rows.shape[2]
    batch, share = upstream.shape
    tables = share // columns
    lanes = cap * columns
    highs = rows_dev // LANES
    ids = unique_rows[:, 0, :].T
    emb = embedding.T.reshape(columns, highs, LANES).transpose(1, 0, 2).reshape(highs * columns, LANES)
    picked = pick(ids, emb, owners, lanes)
    arrived = lax.all_to_all(picked, "table", 0, 0, tiled=True)
    counts = count(lookup_slot, bag_of_lookup, cap, tables, batch * tables, owners * cap)
    rows = lax.all_to_all(
        jnp.broadcast_to(arrived[None], (cuts,) + arrived.shape), "cuts", 0, 0, tiled=True
    )
    own = lax.axis_index("cuts").astype(jnp.int32).reshape(1)
    cross_out, grads = cross(own, rows, counts, cross_weight, cross_bias.reshape(1, share), upstream, cap)
    grads = lax.all_to_all(grads, "cuts", 0, 0, tiled=True)
    grads = jnp.sum(grads.astype(jnp.float32), axis=0).astype(jnp.bfloat16)
    returned = lax.all_to_all(grads, "table", 0, 0, tiled=True)
    row_grads = scatter(ids, returned, highs * columns)
    row_grads = row_grads.reshape(highs, columns, LANES).transpose(1, 0, 2).reshape(columns, rows_dev).T
    return cross_out, row_grads


def solution(mesh):
    return jax.shard_map(
        per_device,
        mesh=mesh,
        in_specs=(
            P("table", "cuts"),
            P(None, "cuts"),
            P("cuts"),
            P("table", "cuts"),
            P(None, "table", None),
            P("table", None),
            P("table", None),
        ),
        out_specs=(P("table", "cuts"), P("table", "cuts")),
        check_vma=False,
    )
```

time: 470 us -> 148 us (0.31)
  waiting for transfers between devices: 222 us -> 0.01 us
  local copies, waits for them, and re-layouts: 103 us -> 4.17 us
  blocking collectives: 0 us -> 95.3 us
  starting transfers between devices: 55.9 us -> 6.75 us
  Pallas kernels: 0 us -> 41 us
  loops' own time: 32.1 us -> 0 us
  other arithmetic: 24.3 us -> 0.04 us
  matrix products: 17.7 us -> 0 us
  between operations: 14.4 us -> 0.71 us
    reduce_scatter x1 -> x0, waiting for transfers between devices: 113 us -> none  [per_device(): lax.psum_scatter(lax.dot_general(weight_rows, mix_grad, (((1,), (1,)), ((...]
    all_to_all x0 -> x3, blocking collectives: none -> 95.3 us  [the longest x1 52.6 us: per_device(): arrived = lax.all_to_all(picked, 'table', 0, 0, tiled=True)]
    gather x6 -> x0, local copies, waits for them, and re-layouts: 69.2 us -> none  [the longest x2 32.2 us: per_device(): jnp.take(base_grad.reshape(bag_count, columns), bag_index, axis=0)]
    all_gather x1 -> x0, waiting for transfers between devices: 57.4 us -> none  [per_device(): lax.all_gather(local_base, 'cuts', axis=1, tiled=True)]
    all_to_all x2 -> x1, waiting for transfers between devices: 50.9 us -> 0.01 us  [per_device(): lax.all_to_all(jnp.broadcast_to(arrived[None], (cuts,) + arrived.shape),...]
    all_to_all x2 -> x1, starting transfers between devices: 55.8 us -> 6.75 us  [per_device(): lax.all_to_all(jnp.broadcast_to(arrived[None], (cuts,) + arrived.shape),...]
    pallas_call x0 -> x4, Pallas kernels: none -> 41 us  [the longest x1 29.5 us: count(): call(functools.partial(count_kernel, cap, tables), jax.ShapeDtypeStruct((...]
    another operation x2 -> x0, loops' own time: 32.1 us -> none  [the longest x1 31.6 us: pool_sorted(): lax.scan(pool_add_block, start, (looked_blocks, bag_blocks))]
  transfers between devices with their start and end apart: 4 -> 1, of which waited for: 4 -> 0; matrix products, arithmetic and copies ran while one was open for 1% -> 0% of each run, Pallas kernels for 0% -> 20%
where the time goes in v1:
time: 148 us
  blocking collectives  95.3 us (64%)
  Pallas kernels  41 us (28%)
  starting transfers between devices  6.75 us (5%)
  local copies, waits for them, and re-layouts  4.17 us (3%)
    all_to_all x1, blocking collectives, per_device(): arrived = lax.all_to_all(picked, 'table', 0, 0, tiled=True)  52.6 us
    pallas_call x1, Pallas kernels, count(): call(functools.partial(count_kernel, cap, tables), jax.ShapeDtypeStruct((...  29.5 us
    all_to_all x1, blocking collectives, per_device(): returned = lax.all_to_all(grads, 'table', 0, 0, tiled=True)  28.7 us
    all_to_all x1, blocking collectives, per_device(): grads = lax.all_to_all(grads, 'cuts', 0, 0, tiled=True)  13.9 us
    pallas_call x1, Pallas kernels, cross(): call(functools.partial(cross_kernel, cap), (jax.ShapeDtypeStruct(up.shape...  8.94 us
    all_to_all x1, starting transfers between devices, per_device(): lax.all_to_all(jnp.broadcast_to(arrived[None], (cuts,) + arrived.shape),...  6.75 us
    unnamed x18, local copies, waits for them, and re-layouts  3.32 us
  transfers between devices with their start and end apart: 1, of which 0 were waited for; matrix products, arithmetic and copies ran while one was open for 0% of the time, Pallas kernels for 20%

profile of v1, /device:TPU:1, one launch (start us, length us, event | category | flops | bytes accessed | tf_op | source)
XLA Modules:
  0.0 147.9 jit_solution(16598105031559659456)
XLA Ops:
  0.6 0.0 copy-start
  0.6 0.0 copy-start.1
  0.6 1.1 copy-done.1
  1.7 0.0 copy-start.5
  1.7 0.7 copy-done.5
  2.4 0.9 shard_map.86
  3.3 0.1 copy.10
  3.4 52.6 %all_to_all.30 = bf16[64,1,128]{2,1,0:T(2,128)(2,1)S(1)} all-to-all(bf16[64,1,128]{2,1,0:T(2,128)(2,1)S(1)} %copy.10), channel_id=1, replica_groups=mesh['table'=64,'cuts'=16] {'table'}, dimensions={0} | all-to-all | bytes 32768 | tf_op jit(solution)/shard_map/all_to_all | solution.py:264
  56.0 0.8 broadcast_in_dim.9
  56.8 6.8 %all-to-all-start.1 = ((bf16[16,64,128]{2,1,0:T(8,128)(2,1)}), bf16[16,64,128]{2,1,0:T(8,128)(2,1)S(1)}, u32[]{:S(2)}, u32[]{:S(2)}) async-start(bf16[16,64,128]{2,1,0:T(8,128)(2,1)} %broadcast_in_dim.9), calls=%async_computation.1 | async-start | bytes 524288 | tf_op jit(solution)/shard_map/all_to_all | solution.py:266
  63.5 0.0 copy-start.2
  63.5 0.7 copy-done.2
  64.3 0.0 copy-start.4
  64.3 0.8 copy-done.4
  65.1 0.0 copy-start.3
  65.1 0.0 copy-start.7
  65.1 0.0 copy-start.6
  65.1 29.5 %shard_map.87.count_ref = bf16[4096,1024]{1,0:T(8,128)(2,1)} custom-call(s32[1,8192]{1,0:T(1,128)S(1)} %copy-done.2, s32[1,8192]{1,0:T(1,128)S(1)} %copy-done.4, s32[1,8192]{1,0:T(1,128)S(1)} %copy-done.2), custom_call_target="tpu_custom_call" | custom-call | tf_op jit(solution)/shard_map/pallas_call | solution.py:227
  94.6 0.0 all-to-all-done.1.rows_ref
  94.6 0.0 copy-done
  94.6 0.0 copy-done.3
  94.6 0.0 copy-done.7
  94.6 8.9 %shard_map.88 = (bf16[128,256]{1,0:T(8,128)(2,1)}, bf16[16,64,128]{2,1,0:T(8,128)(2,1)S(1)}) custom-call(s32[1]{0:T(128)} %bitcast.own_ref, bf16[16,64,128]{2,1,0:T(8,128)(2,1)S(1)} %all-to-all-done.1.rows_ref, bf16[4096,1024]{1,0:T(8,128)(2,1)} %shard_map.87.count_ref, bf16[4096,256]{1,0:T(8,128)(2,1)S(1)} %copy-done, f32[1,256]{1,0:T(1,128)S(1)} %bitcast.32, ...), custom_call_target="tpu_custom_call" | custom-call | tf_op jit(solution)/shard_map/pallas_call | solution.py:240
  103.5 13.9 %all_to_all.31 = bf16[16,64,128]{2,1,0:T(8,128)(2,1)S(1)} all-to-all(bf16[16,64,128]{2,1,0:T(8,128)(2,1)S(1)} %get-tuple-element.5), channel_id=1, replica_groups=mesh['table'=64,'cuts'=16] {'cuts'}, dimensions={0} | all-to-all | bytes 524288 | tf_op jit(solution)/shard_map/all_to_all | solution.py:271
  117.5 28.7 %all_to_all.32 = bf16[64,1,128]{2,1,0:T(2,128)(2,1)S(1)} all-to-all(bf16[64,1,128]{2,1,0:T(2,128)(2,1)S(1)} %copy.11), channel_id=1, replica_groups=mesh['table'=64,'cuts'=16] {'table'}, dimensions={0} | all-to-all | bytes 32768 | tf_op jit(solution)/shard_map/all_to_all | solution.py:273
  146.3 0.0 copy-done.6
  146.3 1.6 %shard_map.89 = f32[1024,128]{1,0:T(8,128)} custom-call(s32[16,64]{1,0:T(8,128)S(1)} %bitcast.31, bf16[64,128]{1,0:T(8,128)(2,1)S(1)} %bitcast.28), custom_call_target="tpu_custom_call" | custom-call | tf_op jit(solution)/shard_map/pallas_call | solution.py:222
  (4 shorter events, 0.1 us)
Async XLA Ops:
  0.6 93.9 %copy-start = (bf16[4096,256]{1,0:T(8,128)(2,1)S(1)}, bf16[4096,256]{1,0:T(8,128)(2,1)}, u32[]{:S(2)}) copy-start(bf16[4096,256]{1,0:T(8,128)(2,1)} %weight_ref.1) | copy-start | bytes 6291460
  0.6 1.1 copy-start.1
  1.7 0.7 copy-start.5
  56.8 37.8 %all-to-all-start.1 = ((bf16[16,64,128]{2,1,0:T(8,128)(2,1)}), bf16[16,64,128]{2,1,0:T(8,128)(2,1)S(1)}, u32[]{:S(2)}, u32[]{:S(2)}) async-start(bf16[16,64,128]{2,1,0:T(8,128)(2,1)} %broadcast_in_dim.9), calls=%async_computation.1 | async-start | bytes 524288 | tf_op jit(solution)/shard_map/all_to_all | solution.py:266
  63.5 0.8 copy-start.2
  64.3 0.8 copy-start.4
  65.1 29.5 %copy-start.3 = (bf16[128,256]{1,0:T(8,128)(2,1)S(1)}, bf16[128,256]{1,0:T(8,128)(2,1)}, u32[]{:S(2)}) copy-start(bf16[128,256]{1,0:T(8,128)(2,1)} %up_ref.1) | copy-start | bytes 196612
  65.1 29.5 %copy-start.7 = (f32[256]{0:T(256)S(1)}, f32[256]{0:T(256)}, u32[]{:S(2)}) copy-start(f32[256]{0:T(256)} %param.9) | copy-start | bytes 3076
  65.1 81.2 %copy-start.6 = (s32[64,1,16]{0,2,1:T(8,128)S(1)}, s32[64,1,16]{0,2,1:T(8,128)}, u32[]{:S(2)}) copy-start(s32[64,1,16]{0,2,1:T(8,128)} %param.11) | copy-start | bytes 12292

commit v2 on v1

--- a/solution.py
+++ b/solution.py
@@ -9,7 +9,6 @@
 
 LANES = 128
 LOOK_BLOCK = 256
-WINDOW = LOOK_BLOCK + 8
 NT = (((1,), (1,)), ((), ()))
 
 
@@ -19,6 +18,14 @@
 
 def dot_nt(a, b):
     return lax.dot_general(a, b, NT, preferred_element_type=jnp.float32)
+
+
+def one_hot(hit):
+    return hit.astype(jnp.float32).astype(jnp.bfloat16)
+
+
+def window_rows(tables, pitch):
+    return (LOOK_BLOCK + 7 + (LOOK_BLOCK // tables + 1) * (pitch - tables) + 7) // 8 * 8
 
 
 def swap_blocks(parts, width):
@@ -46,7 +53,13 @@
     return ids // LANES, ids % LANES
 
 
-def pick_kernel(ids_ref, emb_ref, out_ref):
+def pick_kernel(ids_hbm, emb_hbm, out_ref, ids_ref, emb_ref, ids_sem, emb_sem):
+    emb_copy = pltpu.make_async_copy(emb_hbm, emb_ref, emb_sem)
+    ids_copy = pltpu.make_async_copy(ids_hbm, ids_ref, ids_sem)
+    emb_copy.start()
+    ids_copy.start()
+    ids_copy.wait()
+    emb_copy.wait()
     cap, shards = ids_ref.shape
     columns = out_ref.shape[1] // cap
     highs = emb_ref.shape[0] // columns
@@ -55,7 +68,7 @@
     for group in range(cap // per):
         hi, lo = row_halves(ids_ref, group, per)
         n = hi.shape[1]
-        low_hot = (lax.broadcasted_iota(jnp.int32, (LANES, n), 0) == lo).astype(jnp.float32).astype(jnp.bfloat16)
+        low_hot = one_hot(lax.broadcasted_iota(jnp.int32, (LANES, n), 0) == lo)
         wide = dot(emb_ref[...], low_hot).reshape(highs, columns, n)
         high_hot = lax.broadcasted_iota(jnp.int32, (highs, columns, n), 0) == hi[None]
         found = jnp.sum(jnp.where(high_hot, wide, 0.0), axis=0)
@@ -73,7 +86,7 @@
     for group in range(cap // per):
         hi, lo = row_halves(ids_ref, group, per)
         n = hi.shape[1]
-        low_hot = (lax.broadcasted_iota(jnp.int32, (LANES, n), 0) == lo).astype(jnp.float32).astype(jnp.bfloat16)
+        low_hot = one_hot(lax.broadcasted_iota(jnp.int32, (LANES, n), 0) == lo)
         values = jnp.concatenate(
             [turned[(group * per + k) * columns : (group * per + k + 1) * columns] for k in range(per)],
             axis=1,
@@ -87,48 +100,78 @@
             out_ref[...] += part
 
 
-def count_kernel(cap, tables, firsts_ref, slot_ref, bag_ref, out_ref, acc):
+def count_kernel(cap, owners, tables, pitch, first_slot, firsts_ref, slot_ref, bag_ref, out_hbm, acc, out_ref, sems):
     look = slot_ref.shape[1]
     slots = out_ref.shape[1]
-    owners = slots // cap
     batch = out_ref.shape[0] // tables
+    gap = pitch - tables
+    window = window_rows(tables, pitch)
     for n in range(slots // LANES):
         acc[n, 0:8, :] = jnp.zeros((8, LANES), jnp.float32)
 
     def body(i, carry):
         at = pl.ds(pl.multiple_of(i * LOOK_BLOCK, LOOK_BLOCK), LOOK_BLOCK)
-        start = pl.multiple_of(firsts_ref[0, i * LOOK_BLOCK] // 8 * 8, 8)
-        bags = bag_ref[:, at] - start
+        first = firsts_ref[0, i * LOOK_BLOCK]
+        start = pl.multiple_of((first + first // tables * gap) // 8 * 8, 8)
+        bags = bag_ref[:, at]
+        bags = bags + bags // tables * gap - start
         slot = slot_ref[:, at]
-        order = slot % cap * owners + slot // cap
-        bag_hot = (lax.broadcasted_iota(jnp.int32, (WINDOW, LOOK_BLOCK), 0) == bags).astype(jnp.float32).astype(jnp.bfloat16)
+        order = slot % cap * owners + slot // cap - first_slot
+        bag_hot = one_hot(lax.broadcasted_iota(jnp.int32, (window, LOOK_BLOCK), 0) == bags)
         for n in range(slots // 256):
-            slot_hot = (
-                (lax.broadcasted_iota(jnp.int32, (256, LOOK_BLOCK), 0) + n * 256 == order)
-                .astype(jnp.float32)
-                .astype(jnp.bfloat16)
-            )
+            slot_hot = one_hot(lax.broadcasted_iota(jnp.int32, (256, LOOK_BLOCK), 0) + n * 256 == order)
             part = dot_nt(bag_hot, slot_hot)
             for m in range(2):
                 cols = slice(m * LANES, (m + 1) * LANES)
                 acc[2 * n + m, pl.ds(start, 8), :] += part[0:8, cols]
-                acc[2 * n + m, pl.ds(start + 8, WINDOW - 8), :] = part[8:, cols]
+                acc[2 * n + m, pl.ds(start + 8, window - 8), :] = part[8:, cols]
         return carry
 
-    lax.fori_loop(0, look // LOOK_BLOCK, body, 0)
-    for f in range(tables):
-        row = (f % 2 * (tables // 2) + f // 2) * batch
+    lax.fori_loop(0, look // LOOK_BLOCK, body, 0, unroll=4)
+    chunks = sems.shape[0]
+    copies = []
+    for place in range(tables):
+        half = tables // 2
+        f = place % half * 2 + place // half
+        row = place * batch
         for n in range(slots // LANES):
             cols = slice(n * LANES, (n + 1) * LANES)
-            out_ref[row : row + batch, cols] = acc[n, pl.ds(f, batch, stride=tables), :].astype(jnp.bfloat16)
-
-
-def cross_kernel(cap, own_ref, rows_ref, count_ref, weight_ref, bias_ref, up_ref, out_ref, grad_ref, base_s, turned_s):
+            out_ref[row : row + batch, cols] = acc[n, pl.ds(f, batch, stride=pitch), :].astype(jnp.bfloat16)
+        if (place + 1) % (tables // chunks) == 0:
+            done = pl.ds(len(copies) * (out_ref.shape[0] // chunks), out_ref.shape[0] // chunks)
+            copies.append(pltpu.make_async_copy(out_ref.at[done], out_hbm.at[done], sems.at[len(copies)]))
+            copies[-1].start()
+    for copy in copies:
+        copy.wait()
+
+
+def cross_kernel(
+    cap, own_ref, rows_ref, low_hbm, high_hbm, weight_ref, bias_ref, up_ref, out_ref, grad_ref,
+    count_ref, base_s, turned_s, sems,
+):
     cuts, owners, lanes = rows_ref.shape
     columns = lanes // cap
     batch, share = up_ref.shape
     pairs = share // (2 * columns)
     own = own_ref[0]
+    half = pairs * batch
+    chunk = 4 * batch
+    width = low_hbm.shape[1]
+    copies = []
+    for c in range(half // chunk):
+        for k, (source, at, left) in enumerate(
+            (source, side + c * chunk, left)
+            for side in (0, half)
+            for source, left in ((low_hbm, 0), (high_hbm, width))
+        ):
+            copies.append(
+                pltpu.make_async_copy(
+                    source.at[pl.ds(at, chunk)],
+                    count_ref.at[pl.ds(at, chunk), pl.ds(left, width)],
+                    sems.at[c * 4 + k],
+                )
+            )
+            copies[-1].start()
 
     picked = swap_blocks([rows_ref[q].astype(jnp.float32) for q in range(cuts)], columns)
     rows = jnp.concatenate(picked, axis=0).astype(jnp.bfloat16)
@@ -142,10 +185,10 @@
     rows_even = dot(rows, put_even).astype(jnp.bfloat16)
     rows_odd = dot(rows, put_odd).astype(jnp.bfloat16)
 
-    half = pairs * batch
-    chunk = 4 * batch
     for c in range(half // chunk):
         at = c * chunk
+        for copy in copies[c * 4 : c * 4 + 4]:
+            copy.wait()
         both = dot(count_ref[at : at + chunk, :], rows_even) + dot(
             count_ref[half + at : half + at + chunk, :], rows_odd
         )
@@ -199,8 +242,8 @@
         grad_ref[q] = parts[q].astype(jnp.bfloat16)
 
 
-def call(kernel, out_shape, in_spaces, scratch=(), limit=48, **kw):
-    outs = jax.tree.map(lambda unused: pl.BlockSpec(memory_space=pltpu.VMEM), out_shape)
+def call(kernel, out_shape, in_spaces, scratch=(), limit=48, out_space=pltpu.VMEM, **kw):
+    outs = jax.tree.map(lambda unused: pl.BlockSpec(memory_space=out_space), out_shape)
     return pl.pallas_call(
         kernel,
         out_shape=out_shape,
@@ -213,40 +256,61 @@
 
 
 def pick(ids, emb, shards, lanes, **kw):
-    V = pltpu.VMEM
-    return call(pick_kernel, jax.ShapeDtypeStruct((shards, lanes), jnp.bfloat16), [V, V], **kw)(ids, emb)
+    scratch = [
+        pltpu.VMEM(ids.shape, ids.dtype),
+        pltpu.VMEM(emb.shape, emb.dtype),
+        pltpu.SemaphoreType.DMA,
+        pltpu.SemaphoreType.DMA,
+    ]
+    out = jax.ShapeDtypeStruct((shards, lanes), jnp.bfloat16)
+    return call(pick_kernel, out, [pltpu.HBM, pltpu.HBM], scratch, limit=62, **kw)(ids, emb)
 
 
 def scatter(ids, grads, rows_out, **kw):
     V = pltpu.VMEM
-    return call(scatter_kernel, jax.ShapeDtypeStruct((rows_out, LANES), jnp.float32), [V, V], **kw)(ids, grads)
-
-
-def count(slot, bag, cap, tables, bags, slots, **kw):
+    return call(scatter_kernel, jax.ShapeDtypeStruct((rows_out, LANES), jnp.float32), [V, V], limit=16, **kw)(ids, grads)
+
+
+def count(slot, bag, cap, tables, bags, slots, side, **kw):
     V, S = pltpu.VMEM, pltpu.SMEM
+    pitch = tables + 1
+    rows = (bags // tables - 1) * pitch + tables + window_rows(tables, pitch)
+    rows = (rows + 7) // 8 * 8
+    width = slots // 2
+    out = jax.ShapeDtypeStruct((bags, width), jnp.bfloat16)
     return call(
-        functools.partial(count_kernel, cap, tables),
-        jax.ShapeDtypeStruct((bags, slots), jnp.bfloat16),
+        functools.partial(count_kernel, cap, slots // cap, tables, pitch, side * width),
+        out,
         [S, V, V],
-        [pltpu.VMEM((slots // LANES, bags + WINDOW, LANES), jnp.float32)],
+        [
+            pltpu.VMEM((width // LANES, rows, LANES), jnp.float32),
+            pltpu.VMEM(out.shape, out.dtype),
+            pltpu.SemaphoreType.DMA((8,)),
+        ],
+        out_space=pltpu.HBM,
+        limit=58,
         **kw,
     )(bag, slot, bag)
 
 
-def cross(own, rows, counts, weight, bias, up, cap, **kw):
-    V, S = pltpu.VMEM, pltpu.SMEM
+def cross(own, rows, low, high, weight, bias, up, cap, **kw):
+    V, S, H = pltpu.VMEM, pltpu.SMEM, pltpu.HBM
     cuts, owners, lanes = rows.shape
     batch, share = up.shape
+    bags = low.shape[0]
     return call(
         functools.partial(cross_kernel, cap),
         (jax.ShapeDtypeStruct(up.shape, jnp.bfloat16), jax.ShapeDtypeStruct(rows.shape, jnp.bfloat16)),
-        [S, V, V, V, V, V],
+        [S, V, H, H, V, V, V],
         [
-            pltpu.VMEM((counts.shape[0] // 2, 2 * lanes), jnp.bfloat16),
-            pltpu.VMEM((lanes, counts.shape[0]), jnp.bfloat16),
+            pltpu.VMEM((bags, 2 * low.shape[1]), jnp.bfloat16),
+            pltpu.VMEM((bags // 2, 2 * lanes), jnp.bfloat16),
+            pltpu.VMEM((lanes, bags), jnp.bfloat16),
+            pltpu.SemaphoreType.DMA((bags // (2 * batch),)),
         ],
+        limit=48,
         **kw,
-    )(own, rows, counts, weight, bias, up)
+    )(own, rows, low, high, weight, bias, up)
 
 
 def per_device(embedding, cross_weight, cross_bias, upstream, unique_rows, lookup_slot, bag_of_lookup):
@@ -262,12 +326,17 @@
     emb = embedding.T.reshape(columns, highs, LANES).transpose(1, 0, 2).reshape(highs * columns, LANES)
     picked = pick(ids, emb, owners, lanes)
     arrived = lax.all_to_all(picked, "table", 0, 0, tiled=True)
-    counts = count(lookup_slot, bag_of_lookup, cap, tables, batch * tables, owners * cap)
+    sizes = (cap, tables, batch * tables, owners * cap)
+    low = count(lookup_slot, bag_of_lookup, *sizes, 0)
+    arrived, low, lookup_slot, bag_of_lookup = lax.optimization_barrier(
+        (arrived, low, lookup_slot, bag_of_lookup)
+    )
     rows = lax.all_to_all(
         jnp.broadcast_to(arrived[None], (cuts,) + arrived.shape), "cuts", 0, 0, tiled=True
     )
+    high = count(lookup_slot, bag_of_lookup, *sizes, 1)
     own = lax.axis_index("cuts").astype(jnp.int32).reshape(1)
-    cross_out, grads = cross(own, rows, counts, cross_weight, cross_bias.reshape(1, share), upstream, cap)
+    cross_out, grads = cross(own, rows, low, high, cross_weight, cross_bias.reshape(1, share), upstream, cap)
     grads = lax.all_to_all(grads, "cuts", 0, 0, tiled=True)
     grads = jnp.sum(grads.astype(jnp.float32), axis=0).astype(jnp.bfloat16)
     returned = lax.all_to_all(grads, "table", 0, 0, tiled=True)

time: 148 us -> 129 us (0.87)
  blocking collectives: 95.3 us -> 45.6 us
  starting transfers between devices: 6.75 us -> 37.2 us
  waiting for transfers between devices: 0.01 us -> 14.8 us
  Pallas kernels: 41 us -> 28.4 us
  local copies, waits for them, and re-layouts: 4.17 us -> 2.18 us
    all_to_all x1 -> x0, blocking collectives: 52.6 us -> none  [per_device(): arrived = lax.all_to_all(picked, 'table', 0, 0, tiled=True)]
    all_to_all x0 -> x1, starting transfers between devices: none -> 30.4 us  [per_device(): arrived = lax.all_to_all(picked, 'table', 0, 0, tiled=True)]
    all_to_all x0 -> x1, waiting for transfers between devices: none -> 14.8 us  [per_device(): arrived = lax.all_to_all(picked, 'table', 0, 0, tiled=True)]
    pallas_call x2 -> x3, Pallas kernels: 30.4 us -> 17.5 us  [the longest x2 15 us: count(): call(functools.partial(count_kernel, cap, slots // cap, tables, pitch, si...]
    unnamed x18 -> x10, local copies, waits for them, and re-layouts: 3.32 us -> 0.03 us
    all_to_all x1, blocking collectives: 28.7 us -> 31.7 us  [per_device(): returned = lax.all_to_all(grads, 'table', 0, 0, tiled=True)]
  transfers between devices with their start and end apart: 1 -> 2, of which waited for: 0 -> 1; matrix products, arithmetic and copies ran while one was open for 0% -> 0% of each run, Pallas kernels for 20% -> 12%
where the time goes in v2:
time: 129 us
  blocking collectives  45.6 us (35%)
  starting transfers between devices  37.2 us (29%)
  Pallas kernels  28.4 us (22%)
  waiting for transfers between devices  14.8 us (11%)
  local copies, waits for them, and re-layouts  2.18 us (2%)
    all_to_all x1, blocking collectives, per_device(): returned = lax.all_to_all(grads, 'table', 0, 0, tiled=True)  31.7 us
    all_to_all x1, starting transfers between devices, per_device(): arrived = lax.all_to_all(picked, 'table', 0, 0, tiled=True)  30.4 us
    pallas_call x2, Pallas kernels, count(): call(functools.partial(count_kernel, cap, slots // cap, tables, pitch, si...  15 us
    all_to_all x1, waiting for transfers between devices, per_device(): arrived = lax.all_to_all(picked, 'table', 0, 0, tiled=True)  14.8 us
    all_to_all x1, blocking collectives, per_device(): grads = lax.all_to_all(grads, 'cuts', 0, 0, tiled=True)  13.9 us
    pallas_call x1, Pallas kernels, cross(): call(functools.partial(cross_kernel, cap), (jax.ShapeDtypeStruct(up.shape...  9.26 us
    all_to_all x1, starting transfers between devices, per_device(): lax.all_to_all(jnp.broadcast_to(arrived[None], (cuts,) + arrived.shape),...  6.75 us
  transfers between devices with their start and end apart: 2, of which 1 were waited for; matrix products, arithmetic and copies ran while one was open for 0% of the time, Pallas kernels for 12%

profile of v2, /device:TPU:1, one launch (start us, length us, event | category | flops | bytes accessed | tf_op | source)
XLA Modules:
  0.0 128.8 jit_solution(4355456943281770665)
XLA Ops:
  0.6 2.5 %shard_map.86 = bf16[64,128]{1,0:T(8,128)(2,1)} custom-call(s32[16,64]{1,0:T(8,128)} %bitcast.28, bf16[1024,128]{1,0:T(8,128)(2,1)} %bitcast.32), custom_call_target="tpu_custom_call" | custom-call | tf_op jit(solution)/shard_map/pallas_call | solution.py:266
  3.1 1.4 %copy.10 = bf16[64,1,128]{2,1,0:T(2,128)(2,1)} copy(bf16[64,1,128]{2,0,1:T(8,128)(2,1)} %bitcast.35) | data formatting | bytes 32768 | tf_op jit(solution)/shard_map/all_to_all | solution.py:328
  4.5 30.4 %all-to-all-start = ((bf16[64,1,128]{2,1,0:T(2,128)(2,1)}), bf16[64,1,128]{2,1,0:T(2,128)(2,1)S(1)}, u32[]{:S(2)}, u32[]{:S(2)}) async-start(bf16[64,1,128]{2,1,0:T(2,128)(2,1)} %copy.10), calls=%async_computation | async-start | bytes 65536 | tf_op jit(solution)/shard_map/all_to_all | solution.py:328
  34.9 0.0 copy-start
  34.9 0.0 copy-start.1
  34.9 0.0 copy-start.3
  34.9 7.5 %shard_map.87.low_hbm = bf16[4096,512]{1,0:T(8,128)(2,1)} custom-call(s32[1,8192]{1,0:T(1,128)} %bag_ref.2, s32[1,8192]{1,0:T(1,128)} %slot_ref.2, s32[1,8192]{1,0:T(1,128)} %bag_ref.2), custom_call_target="tpu_custom_call" | custom-call | tf_op jit(solution)/shard_map/pallas_call | solution.py:281
  42.5 14.8 %all-to-all-done = bf16[64,1,128]{2,1,0:T(2,128)(2,1)S(1)} async-done(((bf16[64,1,128]{2,1,0:T(2,128)(2,1)}), bf16[64,1,128]{2,1,0:T(2,128)(2,1)S(1)}, u32[]{:S(2)}, u32[]{:S(2)}) %all-to-all-start) | async-done | bytes 16416 | tf_op jit(solution)/shard_map/all_to_all | solution.py:328
  57.2 0.8 broadcast_in_dim.2
  58.0 6.8 %all-to-all-start.1 = ((bf16[16,64,128]{2,1,0:T(8,128)(2,1)}), bf16[16,64,128]{2,1,0:T(8,128)(2,1)S(1)}, u32[]{:S(2)}, u32[]{:S(2)}) async-start(bf16[16,64,128]{2,1,0:T(8,128)(2,1)} %broadcast_in_dim.2), calls=%async_computation.1 | async-start | bytes 524288 | tf_op jit(solution)/shard_map/all_to_all | solution.py:334
  64.8 7.4 %shard_map.88.high_hbm = bf16[4096,512]{1,0:T(8,128)(2,1)} custom-call(s32[1,8192]{1,0:T(1,128)} %bag_ref.2, s32[1,8192]{1,0:T(1,128)} %slot_ref.2, s32[1,8192]{1,0:T(1,128)} %bag_ref.2), custom_call_target="tpu_custom_call" | custom-call | tf_op jit(solution)/shard_map/pallas_call | solution.py:281
  72.2 0.0 all-to-all-done.1.rows_ref
  72.2 0.0 copy-done
  72.2 0.0 copy-done.1
  72.2 0.0 copy-done.3
  72.2 0.0 copy-start.2
  72.3 9.3 %shard_map.89 = (bf16[128,256]{1,0:T(8,128)(2,1)}, bf16[16,64,128]{2,1,0:T(8,128)(2,1)S(1)}) custom-call(s32[1]{0:T(128)} %bitcast.own_ref, bf16[16,64,128]{2,1,0:T(8,128)(2,1)S(1)} %all-to-all-done.1.rows_ref, bf16[4096,512]{1,0:T(8,128)(2,1)} %shard_map.87.low_hbm, bf16[4096,512]{1,0:T(8,128)(2,1)} %shard_map.88.high_hbm, bf16[4096,256]{1,0:T(8,128)(2,1)S(1)} %copy-done, ...), custom_call_target="tpu_custom_call" | custom-call | tf_op jit(solution)/shard_map/pallas_call | solution.py:301
  81.5 13.9 %all_to_all.33 = bf16[16,64,128]{2,1,0:T(8,128)(2,1)S(1)} all-to-all(bf16[16,64,128]{2,1,0:T(8,128)(2,1)S(1)} %get-tuple-element.13), channel_id=1, replica_groups=mesh['table'=64,'cuts'=16] {'cuts'}, dimensions={0} | all-to-all | bytes 524288 | tf_op jit(solution)/shard_map/all_to_all | solution.py:340
  95.5 31.7 %all_to_all.34 = bf16[64,1,128]{2,1,0:T(2,128)(2,1)S(1)} all-to-all(bf16[64,1,128]{2,1,0:T(2,128)(2,1)S(1)} %copy.11), channel_id=1, replica_groups=mesh['table'=64,'cuts'=16] {'table'}, dimensions={0} | all-to-all | bytes 32768 | tf_op jit(solution)/shard_map/all_to_all | solution.py:342
  127.2 0.0 copy-done.2
  127.2 1.6 %shard_map.90 = f32[1024,128]{1,0:T(8,128)} custom-call(s32[16,64]{1,0:T(8,128)S(1)} %bitcast.29, bf16[64,128]{1,0:T(8,128)(2,1)S(1)} %bitcast.27), custom_call_target="tpu_custom_call" | custom-call | tf_op jit(solution)/shard_map/pallas_call | solution.py:271
  (4 shorter events, 0.1 us)
Async XLA Ops:
  4.5 52.8 %all-to-all-start = ((bf16[64,1,128]{2,1,0:T(2,128)(2,1)}), bf16[64,1,128]{2,1,0:T(2,128)(2,1)S(1)}, u32[]{:S(2)}, u32[]{:S(2)}) async-start(bf16[64,1,128]{2,1,0:T(2,128)(2,1)} %copy.10), calls=%async_computation | async-start | bytes 65536 | tf_op jit(solution)/shard_map/all_to_all | solution.py:328
  34.9 37.3 %copy-start = (bf16[4096,256]{1,0:T(8,128)(2,1)S(1)}, bf16[4096,256]{1,0:T(8,128)(2,1)}, u32[]{:S(2)}) copy-start(bf16[4096,256]{1,0:T(8,128)(2,1)} %weight_ref.1) | copy-start | bytes 6291460
  34.9 37.3 %copy-start.1 = (bf16[128,256]{1,0:T(8,128)(2,1)S(1)}, bf16[128,256]{1,0:T(8,128)(2,1)}, u32[]{:S(2)}) copy-start(bf16[128,256]{1,0:T(8,128)(2,1)} %up_ref.1) | copy-start | bytes 196612
  34.9 37.3 %copy-start.3 = (f32[256]{0:T(256)S(1)}, f32[256]{0:T(256)}, u32[]{:S(2)}) copy-start(f32[256]{0:T(256)} %param.9) | copy-start | bytes 3076
  58.0 14.2 %all-to-all-start.1 = ((bf16[16,64,128]{2,1,0:T(8,128)(2,1)}), bf16[16,64,128]{2,1,0:T(8,128)(2,1)S(1)}, u32[]{:S(2)}, u32[]{:S(2)}) async-start(bf16[16,64,128]{2,1,0:T(8,128)(2,1)} %broadcast_in_dim.2), calls=%async_computation.1 | async-start | bytes 524288 | tf_op jit(solution)/shard_map/all_to_all | solution.py:334
  72.2 54.9 %copy-start.2 = (s32[64,1,16]{0,2,1:T(8,128)S(1)}, s32[64,1,16]{0,2,1:T(8,128)}, u32[]{:S(2)}) copy-start(s32[64,1,16]{0,2,1:T(8,128)} %param.11) | copy-start | bytes 12292

commit v3 on v2

--- a/solution.py
+++ b/solution.py
@@ -9,6 +9,7 @@
 
 LANES = 128
 LOOK_BLOCK = 256
+UNROLL = 8
 NT = (((1,), (1,)), ((), ()))
 
 
@@ -25,7 +26,7 @@
 
 
 def window_rows(tables, pitch):
-    return (LOOK_BLOCK + 7 + (LOOK_BLOCK // tables + 1) * (pitch - tables) + 7) // 8 * 8
+    return (LOOK_BLOCK + 8 + (LOOK_BLOCK // tables + 1) * (pitch - tables) + 7) // 8 * 8
 
 
 def swap_blocks(parts, width):
@@ -61,7 +62,7 @@
     ids_copy.wait()
     emb_copy.wait()
     cap, shards = ids_ref.shape
-    columns = out_ref.shape[1] // cap
+    columns = out_ref.shape[2] // cap
     highs = emb_ref.shape[0] // columns
     per = 256 // shards
     pieces = []
@@ -74,7 +75,7 @@
         found = jnp.sum(jnp.where(high_hot, wide, 0.0), axis=0)
         for k in range(per):
             pieces.append(found[:, k * shards : (k + 1) * shards])
-    out_ref[...] = jnp.concatenate(pieces, axis=0).T.astype(out_ref.dtype)
+    out_ref[:, 0, :] = jnp.concatenate(pieces, axis=0).T.astype(out_ref.dtype)
 
 
 def scatter_kernel(ids_ref, grad_ref, out_ref):
@@ -100,7 +101,23 @@
             out_ref[...] += part
 
 
-def count_kernel(cap, owners, tables, pitch, first_slot, firsts_ref, slot_ref, bag_ref, out_hbm, acc, out_ref, sems):
+def low_kernel(cap, owners, tables, pitch, firsts_ref, slot_ref, bag_ref, out_hbm, acc, out_ref, sems):
+    rows = out_ref.shape[0] // sems.shape[0]
+    copies = []
+    for c in range(sems.shape[0]):
+        done = pl.ds(c * rows, rows)
+        copies.append(pltpu.make_async_copy(out_ref.at[done], out_hbm.at[done], sems.at[c]))
+
+    def flush(row):
+        if row % rows == 0:
+            copies[row // rows - 1].start()
+
+    count_slots(cap, owners, tables, pitch, 0, firsts_ref, slot_ref, bag_ref, out_ref, acc, flush)
+    for copy in copies:
+        copy.wait()
+
+
+def count_slots(cap, owners, tables, pitch, first_slot, firsts_ref, slot_ref, bag_ref, out_ref, acc, flush):
     look = slot_ref.shape[1]
     slots = out_ref.shape[1]
     batch = out_ref.shape[0] // tables
@@ -127,27 +144,20 @@
                 acc[2 * n + m, pl.ds(start + 8, window - 8), :] = part[8:, cols]
         return carry
 
-    lax.fori_loop(0, look // LOOK_BLOCK, body, 0, unroll=4)
-    chunks = sems.shape[0]
-    copies = []
+    lax.fori_loop(0, look // LOOK_BLOCK, body, 0, unroll=UNROLL)
+    half = tables // 2
     for place in range(tables):
-        half = tables // 2
         f = place % half * 2 + place // half
         row = place * batch
         for n in range(slots // LANES):
             cols = slice(n * LANES, (n + 1) * LANES)
             out_ref[row : row + batch, cols] = acc[n, pl.ds(f, batch, stride=pitch), :].astype(jnp.bfloat16)
-        if (place + 1) % (tables // chunks) == 0:
-            done = pl.ds(len(copies) * (out_ref.shape[0] // chunks), out_ref.shape[0] // chunks)
-            copies.append(pltpu.make_async_copy(out_ref.at[done], out_hbm.at[done], sems.at[len(copies)]))
-            copies[-1].start()
-    for copy in copies:
-        copy.wait()
+        flush(row + batch)
 
 
 def cross_kernel(
-    cap, own_ref, rows_ref, low_hbm, high_hbm, weight_ref, bias_ref, up_ref, out_ref, grad_ref,
-    count_ref, base_s, turned_s, sems,
+    cap, tables, pitch, own_ref, firsts_ref, slot_ref, bag_ref, low_hbm, rows_ref, weight_ref, bias_ref, up_ref,
+    out_ref, grad_ref, count_ref, acc, base_s, turned_s, low_sem,
 ):
     cuts, owners, lanes = rows_ref.shape
     columns = lanes // cap
@@ -156,22 +166,14 @@
     own = own_ref[0]
     half = pairs * batch
     chunk = 4 * batch
+
     width = low_hbm.shape[1]
-    copies = []
-    for c in range(half // chunk):
-        for k, (source, at, left) in enumerate(
-            (source, side + c * chunk, left)
-            for side in (0, half)
-            for source, left in ((low_hbm, 0), (high_hbm, width))
-        ):
-            copies.append(
-                pltpu.make_async_copy(
-                    source.at[pl.ds(at, chunk)],
-                    count_ref.at[pl.ds(at, chunk), pl.ds(left, width)],
-                    sems.at[c * 4 + k],
-                )
-            )
-            copies[-1].start()
+    low_copy = pltpu.make_async_copy(low_hbm, count_ref.at[:, pl.ds(0, width)], low_sem)
+    low_copy.start()
+    high = count_ref.at[:, pl.ds(width, width)]
+    count_slots(
+        cap, owners, tables, pitch, width, firsts_ref, slot_ref, bag_ref, high, acc, lambda row: None
+    )
 
     picked = swap_blocks([rows_ref[q].astype(jnp.float32) for q in range(cuts)], columns)
     rows = jnp.concatenate(picked, axis=0).astype(jnp.bfloat16)
@@ -185,10 +187,9 @@
     rows_even = dot(rows, put_even).astype(jnp.bfloat16)
     rows_odd = dot(rows, put_odd).astype(jnp.bfloat16)
 
+    low_copy.wait()
     for c in range(half // chunk):
         at = c * chunk
-        for copy in copies[c * 4 : c * 4 + 4]:
-            copy.wait()
         both = dot(count_ref[at : at + chunk, :], rows_even) + dot(
             count_ref[half + at : half + at + chunk, :], rows_odd
         )
@@ -262,7 +263,7 @@
         pltpu.SemaphoreType.DMA,
         pltpu.SemaphoreType.DMA,
     ]
-    out = jax.ShapeDtypeStruct((shards, lanes), jnp.bfloat16)
+    out = jax.ShapeDtypeStruct((shards, 1, lanes), jnp.bfloat16)
     return call(pick_kernel, out, [pltpu.HBM, pltpu.HBM], scratch, limit=62, **kw)(ids, emb)
 
 
@@ -271,46 +272,48 @@
     return call(scatter_kernel, jax.ShapeDtypeStruct((rows_out, LANES), jnp.float32), [V, V], limit=16, **kw)(ids, grads)
 
 
-def count(slot, bag, cap, tables, bags, slots, side, **kw):
-    V, S = pltpu.VMEM, pltpu.SMEM
+def count_scratch(slots, bags, tables):
     pitch = tables + 1
     rows = (bags // tables - 1) * pitch + tables + window_rows(tables, pitch)
     rows = (rows + 7) // 8 * 8
-    width = slots // 2
-    out = jax.ShapeDtypeStruct((bags, width), jnp.bfloat16)
+    return pitch, pltpu.VMEM((slots // LANES, rows, LANES), jnp.float32)
+
+
+def count_low(slot, bag, cap, tables, bags, slots, **kw):
+    V, S = pltpu.VMEM, pltpu.SMEM
+    out = jax.ShapeDtypeStruct((bags, slots // 2), jnp.bfloat16)
+    pitch, acc = count_scratch(slots // 2, bags, tables)
     return call(
-        functools.partial(count_kernel, cap, slots // cap, tables, pitch, side * width),
+        functools.partial(low_kernel, cap, slots // cap, tables, pitch),
         out,
         [S, V, V],
-        [
-            pltpu.VMEM((width // LANES, rows, LANES), jnp.float32),
-            pltpu.VMEM(out.shape, out.dtype),
-            pltpu.SemaphoreType.DMA((8,)),
-        ],
+        [acc, pltpu.VMEM(out.shape, out.dtype), pltpu.SemaphoreType.DMA((8,))],
         out_space=pltpu.HBM,
         limit=58,
         **kw,
     )(bag, slot, bag)
 
 
-def cross(own, rows, low, high, weight, bias, up, cap, **kw):
-    V, S, H = pltpu.VMEM, pltpu.SMEM, pltpu.HBM
+def cross(own, slot, bag, low, rows, weight, bias, up, cap, **kw):
+    V, S = pltpu.VMEM, pltpu.SMEM
     cuts, owners, lanes = rows.shape
-    batch, share = up.shape
-    bags = low.shape[0]
+    bags, width = low.shape
+    tables = bags // up.shape[0]
+    pitch, acc = count_scratch(width, bags, tables)
     return call(
-        functools.partial(cross_kernel, cap),
+        functools.partial(cross_kernel, cap, tables, pitch),
         (jax.ShapeDtypeStruct(up.shape, jnp.bfloat16), jax.ShapeDtypeStruct(rows.shape, jnp.bfloat16)),
-        [S, V, H, H, V, V, V],
+        [S, S, V, V, pltpu.HBM, V, V, V, V],
         [
-            pltpu.VMEM((bags, 2 * low.shape[1]), jnp.bfloat16),
+            pltpu.VMEM((bags, 2 * width), jnp.bfloat16),
+            acc,
             pltpu.VMEM((bags // 2, 2 * lanes), jnp.bfloat16),
             pltpu.VMEM((lanes, bags), jnp.bfloat16),
-            pltpu.SemaphoreType.DMA((bags // (2 * batch),)),
+            pltpu.SemaphoreType.DMA,
         ],
         limit=48,
         **kw,
-    )(own, rows, low, high, weight, bias, up)
+    )(own, bag, slot, bag, low, rows, weight, bias, up)
 
 
 def per_device(embedding, cross_weight, cross_bias, upstream, unique_rows, lookup_slot, bag_of_lookup):
@@ -327,16 +330,15 @@
     picked = pick(ids, emb, owners, lanes)
     arrived = lax.all_to_all(picked, "table", 0, 0, tiled=True)
     sizes = (cap, tables, batch * tables, owners * cap)
-    low = count(lookup_slot, bag_of_lookup, *sizes, 0)
-    arrived, low, lookup_slot, bag_of_lookup = lax.optimization_barrier(
-        (arrived, low, lookup_slot, bag_of_lookup)
-    )
+    low = count_low(lookup_slot, bag_of_lookup, *sizes)
+    arrived, low = lax.optimization_barrier((arrived, low))
     rows = lax.all_to_all(
-        jnp.broadcast_to(arrived[None], (cuts,) + arrived.shape), "cuts", 0, 0, tiled=True
-    )
-    high = count(lookup_slot, bag_of_lookup, *sizes, 1)
+        jnp.broadcast_to(arrived.reshape(1, owners, lanes), (cuts, owners, lanes)), "cuts", 0, 0, tiled=True
+    )
     own = lax.axis_index("cuts").astype(jnp.int32).reshape(1)
-    cross_out, grads = cross(own, rows, low, high, cross_weight, cross_bias.reshape(1, share), upstream, cap)
+    cross_out, grads = cross(
+        own, lookup_slot, bag_of_lookup, low, rows, cross_weight, cross_bias.reshape(1, share), upstream, cap
+    )
     grads = lax.all_to_all(grads, "cuts", 0, 0, tiled=True)
     grads = jnp.sum(grads.astype(jnp.float32), axis=0).astype(jnp.bfloat16)
     returned = lax.all_to_all(grads, "table", 0, 0, tiled=True)

time: 129 us -> 127 us (0.984)
  waiting for transfers between devices: 14.8 us -> 23 us
  Pallas kernels: 28.4 us -> 22 us
  blocking collectives: 45.6 us -> 42.5 us
  local copies, waits for them, and re-layouts: 2.18 us -> 0.82 us
    all_to_all x1, waiting for transfers between devices: 0.01 us -> 7.32 us  [per_device(): lax.all_to_all(jnp.broadcast_to(arrived.reshape(1, owners, lanes), (cuts,...]
    pallas_call x3 -> x2, Pallas kernels: 24.2 us -> 17.8 us  [the longest x1 11.1 us: cross(): call(functools.partial(cross_kernel, cap, tables, pitch), (jax.ShapeDtype...]
    all_to_all x1, blocking collectives: 13.9 us -> 10.8 us  [per_device(): grads = lax.all_to_all(grads, 'cuts', 0, 0, tiled=True)]
    all_to_all x1 -> x0, local copies, waits for them, and re-layouts: 1.36 us -> none  [per_device(): arrived = lax.all_to_all(picked, 'table', 0, 0, tiled=True)]
  transfers between devices with their start and end apart: 2 -> 2, of which waited for: 1 -> 2; matrix products, arithmetic and copies ran while one was open for 0% -> 0% of each run, Pallas kernels for 12% -> 5%
where the time goes in v3:
time: 127 us; the launch traced here: 126 us
  blocking collectives  42.5 us (33%)
  starting transfers between devices  37.3 us (29%)
  waiting for transfers between devices  23 us (18%)
  Pallas kernels  22 us (17%)
    all_to_all x1, blocking collectives, per_device(): returned = lax.all_to_all(grads, 'table', 0, 0, tiled=True)  31.7 us
    all_to_all x1, starting transfers between devices, per_device(): arrived = lax.all_to_all(picked, 'table', 0, 0, tiled=True)  30.5 us
    all_to_all x1, waiting for transfers between devices, per_device(): arrived = lax.all_to_all(picked, 'table', 0, 0, tiled=True)  15.7 us
    pallas_call x1, Pallas kernels, cross(): call(functools.partial(cross_kernel, cap, tables, pitch), (jax.ShapeDtype...  11.1 us
    all_to_all x1, blocking collectives, per_device(): grads = lax.all_to_all(grads, 'cuts', 0, 0, tiled=True)  10.8 us
    all_to_all x1, waiting for transfers between devices, per_device(): lax.all_to_all(jnp.broadcast_to(arrived.reshape(1, owners, lanes), (cuts,...  7.32 us
    all_to_all x1, starting transfers between devices, per_device(): lax.all_to_all(jnp.broadcast_to(arrived.reshape(1, owners, lanes), (cuts,...  6.76 us
    pallas_call x1, Pallas kernels, count_low(): call(functools.partial(low_kernel, cap, slots // cap, tables, pitch), out...  6.64 us
  transfers between devices with their start and end apart: 2, of which 2 were waited for; matrix products, arithmetic and copies ran while one was open for 0% of the time, Pallas kernels for 5%

profile of v3, /device:TPU:1, one launch (start us, length us, event | category | flops | bytes accessed | tf_op | source)
XLA Modules:
  0.0 126.4 jit_solution(11751879643688601771)
XLA Ops:
  0.6 0.0 copy-start.1
  0.6 0.0 copy-start.2
  0.7 0.0 copy-start.3
  0.7 0.0 copy-start.5
  0.7 2.6 %shard_map.86 = bf16[64,1,128]{2,1,0:T(2,128)(2,1)} custom-call(s32[16,64]{1,0:T(8,128)} %bitcast.27, bf16[1024,128]{1,0:T(8,128)(2,1)} %bitcast.31), custom_call_target="tpu_custom_call" | custom-call | tf_op jit(solution)/shard_map/pallas_call | solution.py:267
  3.2 0.0 copy-start
  3.2 30.5 %all-to-all-start = ((bf16[64,1,128]{2,1,0:T(2,128)(2,1)}), bf16[64,1,128]{2,1,0:T(2,128)(2,1)S(1)}, u32[]{:S(2)}, u32[]{:S(2)}) async-start(bf16[64,1,128]{2,1,0:T(2,128)(2,1)} %shard_map.86), calls=%async_computation | async-start | bytes 65536 | tf_op jit(solution)/shard_map/all_to_all | solution.py:331
  33.8 6.6 %shard_map.87.low_hbm = bf16[4096,512]{1,0:T(8,128)(2,1)} custom-call(s32[1,8192]{1,0:T(1,128)} %bag_ref.3, s32[1,8192]{1,0:T(1,128)} %slot_ref.3, s32[1,8192]{1,0:T(1,128)} %bag_ref.3), custom_call_target="tpu_custom_call" | custom-call | tf_op jit(solution)/shard_map/pallas_call | solution.py:286
  40.4 15.7 %all-to-all-done = bf16[64,1,128]{2,1,0:T(2,128)(2,1)S(1)} async-done(((bf16[64,1,128]{2,1,0:T(2,128)(2,1)}), bf16[64,1,128]{2,1,0:T(2,128)(2,1)S(1)}, u32[]{:S(2)}, u32[]{:S(2)}) %all-to-all-start) | async-done | bytes 16416 | tf_op jit(solution)/shard_map/all_to_all | solution.py:331
  56.2 0.0 copy-start.4
  56.2 0.8 broadcast_in_dim.8
  56.9 6.8 %all-to-all-start.1 = ((bf16[16,64,128]{2,1,0:T(8,128)(2,1)}), bf16[16,64,128]{2,1,0:T(8,128)(2,1)S(1)}, u32[]{:S(2)}, u32[]{:S(2)}) async-start(bf16[16,64,128]{2,1,0:T(8,128)(2,1)} %broadcast_in_dim.8), calls=%async_computation.1 | async-start | bytes 524288 | tf_op jit(solution)/shard_map/all_to_all | solution.py:335
  63.7 7.3 %all-to-all-done.1.rows_ref = bf16[16,64,128]{2,1,0:T(8,128)(2,1)S(1)} async-done(((bf16[16,64,128]{2,1,0:T(8,128)(2,1)}), bf16[16,64,128]{2,1,0:T(8,128)(2,1)S(1)}, u32[]{:S(2)}, u32[]{:S(2)}) %all-to-all-start.1) | async-done | bytes 262176 | tf_op jit(solution)/shard_map/all_to_all | solution.py:335
  71.0 0.0 copy-done.1
  71.0 0.0 copy-done.2
  71.0 0.0 copy-done.3
  71.0 0.0 copy-done.5
  71.0 0.0 copy-done
  71.0 11.1 %shard_map.88 = (bf16[128,256]{1,0:T(8,128)(2,1)}, bf16[16,64,128]{2,1,0:T(8,128)(2,1)S(1)}) custom-call(s32[1]{0:T(128)} %bitcast.own_ref, s32[1,8192]{1,0:T(1,128)S(1)} %copy-done.1, s32[1,8192]{1,0:T(1,128)S(1)} %copy-done.2, s32[1,8192]{1,0:T(1,128)S(1)} %copy-done.1, bf16[4096,512]{1,0:T(8,128)(2,1)} %shard_map.87.low_hbm, ...), custom_call_target="tpu_custom_call" | custom-call | tf_op jit(solution)/shard_map/pallas_call | solution.py:303
  82.2 10.8 %all_to_all.26 = bf16[16,64,128]{2,1,0:T(8,128)(2,1)S(1)} all-to-all(bf16[16,64,128]{2,1,0:T(8,128)(2,1)S(1)} %get-tuple-element.9), channel_id=1, replica_groups=mesh['table'=64,'cuts'=16] {'cuts'}, dimensions={0} | all-to-all | bytes 524288 | tf_op jit(solution)/shard_map/all_to_all | solution.py:342
  93.1 31.7 %all_to_all.27 = bf16[64,1,128]{2,1,0:T(2,128)(2,1)S(1)} all-to-all(bf16[64,1,128]{2,1,0:T(2,128)(2,1)S(1)} %copy.9), channel_id=1, replica_groups=mesh['table'=64,'cuts'=16] {'table'}, dimensions={0} | all-to-all | bytes 32768 | tf_op jit(solution)/shard_map/all_to_all | solution.py:344
  124.8 0.0 copy-done.4
  124.8 1.6 %shard_map.89 = f32[1024,128]{1,0:T(8,128)} custom-call(s32[16,64]{1,0:T(8,128)S(1)} %bitcast.28, bf16[64,128]{1,0:T(8,128)(2,1)S(1)} %bitcast.26), custom_call_target="tpu_custom_call" | custom-call | tf_op jit(solution)/shard_map/pallas_call | solution.py:272
  (4 shorter events, 0.1 us)
Async XLA Ops:
  0.6 70.4 %copy-start.1 = (s32[1,8192]{1,0:T(1,128)S(1)}, s32[1,8192]{1,0:T(1,128)}, u32[]{:S(2)}) copy-start(s32[1,8192]{1,0:T(1,128)} %bag_ref.3) | copy-start | bytes 98308
  0.6 70.4 %copy-start.2 = (s32[1,8192]{1,0:T(1,128)S(1)}, s32[1,8192]{1,0:T(1,128)}, u32[]{:S(2)}) copy-start(s32[1,8192]{1,0:T(1,128)} %slot_ref.3) | copy-start | bytes 98308
  0.7 70.3 %copy-start.3 = (bf16[128,256]{1,0:T(8,128)(2,1)S(1)}, bf16[128,256]{1,0:T(8,128)(2,1)}, u32[]{:S(2)}) copy-start(bf16[128,256]{1,0:T(8,128)(2,1)} %up_ref.1) | copy-start | bytes 196612
  0.7 70.3 %copy-start.5 = (f32[256]{0:T(256)S(1)}, f32[256]{0:T(256)}, u32[]{:S(2)}) copy-start(f32[256]{0:T(256)} %param.9) | copy-start | bytes 3076
  3.2 67.8 %copy-start = (bf16[4096,256]{1,0:T(8,128)(2,1)S(1)}, bf16[4096,256]{1,0:T(8,128)(2,1)}, u32[]{:S(2)}) copy-start(bf16[4096,256]{1,0:T(8,128)(2,1)} %weight_ref.1) | copy-start | bytes 6291460
  3.2 52.9 %all-to-all-start = ((bf16[64,1,128]{2,1,0:T(2,128)(2,1)}), bf16[64,1,128]{2,1,0:T(2,128)(2,1)S(1)}, u32[]{:S(2)}, u32[]{:S(2)}) async-start(bf16[64,1,128]{2,1,0:T(2,128)(2,1)} %shard_map.86), calls=%async_computation | async-start | bytes 65536 | tf_op jit(solution)/shard_map/all_to_all | solution.py:331
  56.2 68.6 %copy-start.4 = (s32[64,1,16]{0,2,1:T(8,128)S(1)}, s32[64,1,16]{0,2,1:T(8,128)}, u32[]{:S(2)}) copy-start(s32[64,1,16]{0,2,1:T(8,128)} %param.11) | copy-start | bytes 12292
  56.9 14.1 %all-to-all-start.1 = ((bf16[16,64,128]{2,1,0:T(8,128)(2,1)}), bf16[16,64,128]{2,1,0:T(8,128)(2,1)S(1)}, u32[]{:S(2)}, u32[]{:S(2)}) async-start(bf16[16,64,128]{2,1,0:T(8,128)(2,1)} %broadcast_in_dim.8), calls=%async_computation.1 | async-start | bytes 524288 | tf_op jit(solution)/shard_map/all_to_all | solution.py:335

commit v4 on v3

--- a/solution.py
+++ b/solution.py
@@ -101,25 +101,10 @@
             out_ref[...] += part
 
 
-def low_kernel(cap, owners, tables, pitch, firsts_ref, slot_ref, bag_ref, out_hbm, acc, out_ref, sems):
-    rows = out_ref.shape[0] // sems.shape[0]
-    copies = []
-    for c in range(sems.shape[0]):
-        done = pl.ds(c * rows, rows)
-        copies.append(pltpu.make_async_copy(out_ref.at[done], out_hbm.at[done], sems.at[c]))
-
-    def flush(row):
-        if row % rows == 0:
-            copies[row // rows - 1].start()
-
-    count_slots(cap, owners, tables, pitch, 0, firsts_ref, slot_ref, bag_ref, out_ref, acc, flush)
-    for copy in copies:
-        copy.wait()
-
-
-def count_slots(cap, owners, tables, pitch, first_slot, firsts_ref, slot_ref, bag_ref, out_ref, acc, flush):
+def count_kernel(cap, tables, pitch, firsts_ref, slot_ref, bag_ref, out_hbm, acc, out_ref, sems):
     look = slot_ref.shape[1]
     slots = out_ref.shape[1]
+    owners = slots // cap
     batch = out_ref.shape[0] // tables
     gap = pitch - tables
     window = window_rows(tables, pitch)
@@ -133,7 +118,7 @@
         bags = bag_ref[:, at]
         bags = bags + bags // tables * gap - start
         slot = slot_ref[:, at]
-        order = slot % cap * owners + slot // cap - first_slot
+        order = slot % cap * owners + slot // cap
         bag_hot = one_hot(lax.broadcasted_iota(jnp.int32, (window, LOOK_BLOCK), 0) == bags)
         for n in range(slots // 256):
             slot_hot = one_hot(lax.broadcasted_iota(jnp.int32, (256, LOOK_BLOCK), 0) + n * 256 == order)
@@ -146,18 +131,26 @@
 
     lax.fori_loop(0, look // LOOK_BLOCK, body, 0, unroll=UNROLL)
     half = tables // 2
+    chunk = tables // sems.shape[0] * batch
+    copies = []
     for place in range(tables):
         f = place % half * 2 + place // half
         row = place * batch
         for n in range(slots // LANES):
             cols = slice(n * LANES, (n + 1) * LANES)
-            out_ref[row : row + batch, cols] = acc[n, pl.ds(f, batch, stride=pitch), :].astype(jnp.bfloat16)
-        flush(row + batch)
+            counts = acc[n, pl.ds(f, batch, stride=pitch), :]
+            out_ref[row : row + batch, cols] = counts.astype(out_ref.dtype)
+        if (row + batch) % chunk == 0:
+            done = pl.ds(row + batch - chunk, chunk)
+            copies.append(pltpu.make_async_copy(out_ref.at[done], out_hbm.at[done], sems.at[len(copies)]))
+            copies[-1].start()
+    for copy in copies:
+        copy.wait()
 
 
 def cross_kernel(
-    cap, tables, pitch, own_ref, firsts_ref, slot_ref, bag_ref, low_hbm, rows_ref, weight_ref, bias_ref, up_ref,
-    out_ref, grad_ref, count_ref, acc, base_s, turned_s, low_sem,
+    cap, own_ref, count_hbm, rows_ref, weight_ref, bias_ref, up_ref, out_ref, grad_ref,
+    small_ref, count_ref, base_s, turned_s, sems,
 ):
     cuts, owners, lanes = rows_ref.shape
     columns = lanes // cap
@@ -166,14 +159,12 @@
     own = own_ref[0]
     half = pairs * batch
     chunk = 4 * batch
-
-    width = low_hbm.shape[1]
-    low_copy = pltpu.make_async_copy(low_hbm, count_ref.at[:, pl.ds(0, width)], low_sem)
-    low_copy.start()
-    high = count_ref.at[:, pl.ds(width, width)]
-    count_slots(
-        cap, owners, tables, pitch, width, firsts_ref, slot_ref, bag_ref, high, acc, lambda row: None
-    )
+    copies = []
+    for c in range(half // chunk):
+        for side in range(2):
+            part = pl.ds(side * half + c * chunk, chunk)
+            copies.append(pltpu.make_async_copy(count_hbm.at[part], small_ref.at[part], sems.at[2 * c + side]))
+            copies[-1].start()
 
     picked = swap_blocks([rows_ref[q].astype(jnp.float32) for q in range(cuts)], columns)
     rows = jnp.concatenate(picked, axis=0).astype(jnp.bfloat16)
@@ -187,9 +178,13 @@
     rows_even = dot(rows, put_even).astype(jnp.bfloat16)
     rows_odd = dot(rows, put_odd).astype(jnp.bfloat16)
 
-    low_copy.wait()
+    for copy in copies:
+        copy.wait()
     for c in range(half // chunk):
         at = c * chunk
+        for side in range(2):
+            part = slice(side * half + at, side * half + at + chunk)
+            count_ref[part, :] = small_ref[part, :].astype(jnp.bfloat16)
         both = dot(count_ref[at : at + chunk, :], rows_even) + dot(
             count_ref[half + at : half + at + chunk, :], rows_odd
         )
@@ -272,48 +267,46 @@
     return call(scatter_kernel, jax.ShapeDtypeStruct((rows_out, LANES), jnp.float32), [V, V], limit=16, **kw)(ids, grads)
 
 
-def count_scratch(slots, bags, tables):
+def count(slot, bag, cap, tables, bags, slots, **kw):
+    V, S = pltpu.VMEM, pltpu.SMEM
+    out = jax.ShapeDtypeStruct((bags, slots), jnp.int8)
     pitch = tables + 1
     rows = (bags // tables - 1) * pitch + tables + window_rows(tables, pitch)
     rows = (rows + 7) // 8 * 8
-    return pitch, pltpu.VMEM((slots // LANES, rows, LANES), jnp.float32)
-
-
-def count_low(slot, bag, cap, tables, bags, slots, **kw):
-    V, S = pltpu.VMEM, pltpu.SMEM
-    out = jax.ShapeDtypeStruct((bags, slots // 2), jnp.bfloat16)
-    pitch, acc = count_scratch(slots // 2, bags, tables)
     return call(
-        functools.partial(low_kernel, cap, slots // cap, tables, pitch),
+        functools.partial(count_kernel, cap, tables, pitch),
         out,
         [S, V, V],
-        [acc, pltpu.VMEM(out.shape, out.dtype), pltpu.SemaphoreType.DMA((8,))],
+        [
+            pltpu.VMEM((slots // LANES, rows, LANES), jnp.float32),
+            pltpu.VMEM(out.shape, out.dtype),
+            pltpu.SemaphoreType.DMA((8,)),
+        ],
         out_space=pltpu.HBM,
         limit=58,
         **kw,
     )(bag, slot, bag)
 
 
-def cross(own, slot, bag, low, rows, weight, bias, up, cap, **kw):
+def cross(own, counts, rows, weight, bias, up, cap, **kw):
     V, S = pltpu.VMEM, pltpu.SMEM
     cuts, owners, lanes = rows.shape
-    bags, width = low.shape
-    tables = bags // up.shape[0]
-    pitch, acc = count_scratch(width, bags, tables)
+    bags, slots = counts.shape
+    batch = up.shape[0]
     return call(
-        functools.partial(cross_kernel, cap, tables, pitch),
+        functools.partial(cross_kernel, cap),
         (jax.ShapeDtypeStruct(up.shape, jnp.bfloat16), jax.ShapeDtypeStruct(rows.shape, jnp.bfloat16)),
-        [S, S, V, V, pltpu.HBM, V, V, V, V],
+        [S, pltpu.HBM, V, V, V, V],
         [
-            pltpu.VMEM((bags, 2 * width), jnp.bfloat16),
-            acc,
+            pltpu.VMEM(counts.shape, counts.dtype),
+            pltpu.VMEM(counts.shape, jnp.bfloat16),
             pltpu.VMEM((bags // 2, 2 * lanes), jnp.bfloat16),
             pltpu.VMEM((lanes, bags), jnp.bfloat16),
-            pltpu.SemaphoreType.DMA,
+            pltpu.SemaphoreType.DMA((bags // (4 * batch),)),
         ],
         limit=48,
         **kw,
-    )(own, bag, slot, bag, low, rows, weight, bias, up)
+    )(own, counts, rows, weight, bias, up)
 
 
 def per_device(embedding, cross_weight, cross_bias, upstream, unique_rows, lookup_slot, bag_of_lookup):
@@ -330,14 +323,14 @@
     picked = pick(ids, emb, owners, lanes)
     arrived = lax.all_to_all(picked, "table", 0, 0, tiled=True)
     sizes = (cap, tables, batch * tables, owners * cap)
-    low = count_low(lookup_slot, bag_of_lookup, *sizes)
-    arrived, low = lax.optimization_barrier((arrived, low))
+    counts = count(lookup_slot, bag_of_lookup, *sizes)
+    arrived, counts = lax.optimization_barrier((arrived, counts))
     rows = lax.all_to_all(
         jnp.broadcast_to(arrived.reshape(1, owners, lanes), (cuts, owners, lanes)), "cuts", 0, 0, tiled=True
     )
     own = lax.axis_index("cuts").astype(jnp.int32).reshape(1)
     cross_out, grads = cross(
-        own, lookup_slot, bag_of_lookup, low, rows, cross_weight, cross_bias.reshape(1, share), upstream, cap
+        own, counts, rows, cross_weight, cross_bias.reshape(1, share), upstream, cap
     )
     grads = lax.all_to_all(grads, "cuts", 0, 0, tiled=True)
     grads = jnp.sum(grads.astype(jnp.float32), axis=0).astype(jnp.bfloat16)

time: 127 us -> 125 us (0.984)
  blocking collectives: 42.5 us -> 45 us
  waiting for transfers between devices: 23 us -> 20.5 us
  Pallas kernels: 22 us -> 20.5 us
    all_to_all x1, waiting for transfers between devices: 15.7 us -> 13.2 us  [per_device(): arrived = lax.all_to_all(picked, 'table', 0, 0, tiled=True)]
    all_to_all x1, blocking collectives: 31.7 us -> 34.2 us  [per_device(): returned = lax.all_to_all(grads, 'table', 0, 0, tiled=True)]
    pallas_call x2, Pallas kernels: 17.8 us -> 16.3 us  [the longest x1 9.15 us: count(): call(functools.partial(count_kernel, cap, tables, pitch), out, [S, V, V],...]
  transfers between devices with their start and end apart: 2 -> 2, of which waited for: 2 -> 2; matrix products, arithmetic and copies ran while one was open for 0% -> 0% of each run, Pallas kernels for 5% -> 7%
where the time goes in v4:
time: 125 us
  blocking collectives  45 us (36%)
  starting transfers between devices  37.3 us (30%)
  Pallas kernels  20.5 us (16%)
  waiting for transfers between devices  20.5 us (16%)
    all_to_all x1, blocking collectives, per_device(): returned = lax.all_to_all(grads, 'table', 0, 0, tiled=True)  34.2 us
    all_to_all x1, starting transfers between devices, per_device(): arrived = lax.all_to_all(picked, 'table', 0, 0, tiled=True)  30.5 us
    all_to_all x1, waiting for transfers between devices, per_device(): arrived = lax.all_to_all(picked, 'table', 0, 0, tiled=True)  13.2 us
    all_to_all x1, blocking collectives, per_device(): grads = lax.all_to_all(grads, 'cuts', 0, 0, tiled=True)  10.8 us
    pallas_call x1, Pallas kernels, count(): call(functools.partial(count_kernel, cap, tables, pitch), out, [S, V, V],...  9.15 us
    all_to_all x1, waiting for transfers between devices, per_device(): lax.all_to_all(jnp.broadcast_to(arrived.reshape(1, owners, lanes), (cuts,...  7.32 us
    pallas_call x1, Pallas kernels, cross(): call(functools.partial(cross_kernel, cap), (jax.ShapeDtypeStruct(up.shape...  7.19 us
    all_to_all x1, starting transfers between devices, per_device(): lax.all_to_all(jnp.broadcast_to(arrived.reshape(1, owners, lanes), (cuts,...  6.75 us
  transfers between devices with their start and end apart: 2, of which 2 were waited for; matrix products, arithmetic and copies ran while one was open for 0% of the time, Pallas kernels for 7%

profile of v4, /device:TPU:1, one launch (start us, length us, event | category | flops | bytes accessed | tf_op | source)
XLA Modules:
  0.0 124.9 jit_solution(4599253564795694272)
XLA Ops:
  0.6 0.0 copy-start.1
  0.6 0.0 copy-start.3
  0.7 2.6 %shard_map.86 = bf16[64,1,128]{2,1,0:T(2,128)(2,1)} custom-call(s32[16,64]{1,0:T(8,128)} %bitcast.27, bf16[1024,128]{1,0:T(8,128)(2,1)} %bitcast.31), custom_call_target="tpu_custom_call" | custom-call | tf_op jit(solution)/shard_map/pallas_call | solution.py:262
  3.2 0.0 copy-start
  3.2 30.5 %all-to-all-start = ((bf16[64,1,128]{2,1,0:T(2,128)(2,1)}), bf16[64,1,128]{2,1,0:T(2,128)(2,1)S(1)}, u32[]{:S(2)}, u32[]{:S(2)}) async-start(bf16[64,1,128]{2,1,0:T(2,128)(2,1)} %shard_map.86), calls=%async_computation | async-start | bytes 65536 | tf_op jit(solution)/shard_map/all_to_all | solution.py:324
  33.8 9.1 %shard_map.87.count_hbm = s8[4096,1024]{1,0:T(32,128)(4,1)} custom-call(s32[1,8192]{1,0:T(1,128)} %bag_ref.1, s32[1,8192]{1,0:T(1,128)} %slot_ref.1, s32[1,8192]{1,0:T(1,128)} %bag_ref.1), custom_call_target="tpu_custom_call" | custom-call | tf_op jit(solution)/shard_map/pallas_call | solution.py:276
  42.9 13.2 %all-to-all-done = bf16[64,1,128]{2,1,0:T(2,128)(2,1)S(1)} async-done(((bf16[64,1,128]{2,1,0:T(2,128)(2,1)}), bf16[64,1,128]{2,1,0:T(2,128)(2,1)S(1)}, u32[]{:S(2)}, u32[]{:S(2)}) %all-to-all-start) | async-done | bytes 16416 | tf_op jit(solution)/shard_map/all_to_all | solution.py:324
  56.1 0.0 copy-start.2
  56.1 0.8 broadcast_in_dim.8
  56.9 6.8 %all-to-all-start.1 = ((bf16[16,64,128]{2,1,0:T(8,128)(2,1)}), bf16[16,64,128]{2,1,0:T(8,128)(2,1)S(1)}, u32[]{:S(2)}, u32[]{:S(2)}) async-start(bf16[16,64,128]{2,1,0:T(8,128)(2,1)} %broadcast_in_dim.8), calls=%async_computation.1 | async-start | bytes 524288 | tf_op jit(solution)/shard_map/all_to_all | solution.py:328
  63.6 7.3 %all-to-all-done.1.rows_ref = bf16[16,64,128]{2,1,0:T(8,128)(2,1)S(1)} async-done(((bf16[16,64,128]{2,1,0:T(8,128)(2,1)}), bf16[16,64,128]{2,1,0:T(8,128)(2,1)S(1)}, u32[]{:S(2)}, u32[]{:S(2)}) %all-to-all-start.1) | async-done | bytes 262176 | tf_op jit(solution)/shard_map/all_to_all | solution.py:328
  71.0 0.0 copy-done.1
  71.0 0.0 copy-done.3
  71.0 0.0 copy-done
  71.0 7.2 %shard_map.88 = (bf16[128,256]{1,0:T(8,128)(2,1)}, bf16[16,64,128]{2,1,0:T(8,128)(2,1)S(1)}) custom-call(s32[1]{0:T(128)} %bitcast.own_ref, s8[4096,1024]{1,0:T(32,128)(4,1)} %shard_map.87.count_hbm, bf16[16,64,128]{2,1,0:T(8,128)(2,1)S(1)} %all-to-all-done.1.rows_ref, bf16[4096,256]{1,0:T(8,128)(2,1)S(1)} %copy-done, f32[1,256]{1,0:T(1,128)S(1)} %bitcast.29, ...), custom_call_target="tpu_custom_call" | custom-call | tf_op jit(solution)/shard_map/pallas_call | solution.py:296
  78.2 10.8 %all_to_all.26 = bf16[16,64,128]{2,1,0:T(8,128)(2,1)S(1)} all-to-all(bf16[16,64,128]{2,1,0:T(8,128)(2,1)S(1)} %get-tuple-element.9), channel_id=1, replica_groups=mesh['table'=64,'cuts'=16] {'cuts'}, dimensions={0} | all-to-all | bytes 524288 | tf_op jit(solution)/shard_map/all_to_all | solution.py:335
  89.1 34.2 %all_to_all.27 = bf16[64,1,128]{2,1,0:T(2,128)(2,1)S(1)} all-to-all(bf16[64,1,128]{2,1,0:T(2,128)(2,1)S(1)} %copy.9), channel_id=1, replica_groups=mesh['table'=64,'cuts'=16] {'table'}, dimensions={0} | all-to-all | bytes 32768 | tf_op jit(solution)/shard_map/all_to_all | solution.py:337
  123.3 0.0 copy-done.2
  123.3 1.6 %shard_map.89 = f32[1024,128]{1,0:T(8,128)} custom-call(s32[16,64]{1,0:T(8,128)S(1)} %bitcast.28, bf16[64,128]{1,0:T(8,128)(2,1)S(1)} %bitcast.26), custom_call_target="tpu_custom_call" | custom-call | tf_op jit(solution)/shard_map/pallas_call | solution.py:267
  (4 shorter events, 0.1 us)
Async XLA Ops:
  0.6 70.3 %copy-start.1 = (bf16[128,256]{1,0:T(8,128)(2,1)S(1)}, bf16[128,256]{1,0:T(8,128)(2,1)}, u32[]{:S(2)}) copy-start(bf16[128,256]{1,0:T(8,128)(2,1)} %up_ref.1) | copy-start | bytes 196612
  0.6 70.3 %copy-start.3 = (f32[256]{0:T(256)S(1)}, f32[256]{0:T(256)}, u32[]{:S(2)}) copy-start(f32[256]{0:T(256)} %param.9) | copy-start | bytes 3076
  3.2 67.8 %copy-start = (bf16[4096,256]{1,0:T(8,128)(2,1)S(1)}, bf16[4096,256]{1,0:T(8,128)(2,1)}, u32[]{:S(2)}) copy-start(bf16[4096,256]{1,0:T(8,128)(2,1)} %weight_ref.1) | copy-start | bytes 6291460
  3.2 52.9 %all-to-all-start = ((bf16[64,1,128]{2,1,0:T(2,128)(2,1)}), bf16[64,1,128]{2,1,0:T(2,128)(2,1)S(1)}, u32[]{:S(2)}, u32[]{:S(2)}) async-start(bf16[64,1,128]{2,1,0:T(2,128)(2,1)} %shard_map.86), calls=%async_computation | async-start | bytes 65536 | tf_op jit(solution)/shard_map/all_to_all | solution.py:324
  56.1 67.1 %copy-start.2 = (s32[64,1,16]{0,2,1:T(8,128)S(1)}, s32[64,1,16]{0,2,1:T(8,128)}, u32[]{:S(2)}) copy-start(s32[64,1,16]{0,2,1:T(8,128)} %param.11) | copy-start | bytes 12292
  56.9 14.1 %all-to-all-start.1 = ((bf16[16,64,128]{2,1,0:T(8,128)(2,1)}), bf16[16,64,128]{2,1,0:T(8,128)(2,1)S(1)}, u32[]{:S(2)}, u32[]{:S(2)}) async-start(bf16[16,64,128]{2,1,0:T(8,128)(2,1)} %broadcast_in_dim.8), calls=%async_computation.1 | async-start | bytes 524288 | tf_op jit(solution)/shard_map/all_to_all | solution.py:328

commit v5 on v4

--- a/solution.py
+++ b/solution.py
@@ -9,7 +9,7 @@
 
 LANES = 128
 LOOK_BLOCK = 256
-UNROLL = 8
+UNROLL = 16
 NT = (((1,), (1,)), ((), ()))
 
 
@@ -101,10 +101,9 @@
             out_ref[...] += part
 
 
-def count_kernel(cap, tables, pitch, firsts_ref, slot_ref, bag_ref, out_hbm, acc, out_ref, sems):
+def count_kernel(cap, owners, tables, pitch, first_slot, firsts_ref, slot_ref, bag_ref, out_hbm, acc, out_ref, sems):
     look = slot_ref.shape[1]
     slots = out_ref.shape[1]
-    owners = slots // cap
     batch = out_ref.shape[0] // tables
     gap = pitch - tables
     window = window_rows(tables, pitch)
@@ -118,7 +117,7 @@
         bags = bag_ref[:, at]
         bags = bags + bags // tables * gap - start
         slot = slot_ref[:, at]
-        order = slot % cap * owners + slot // cap
+        order = slot % cap * owners + slot // cap - first_slot
         bag_hot = one_hot(lax.broadcasted_iota(jnp.int32, (window, LOOK_BLOCK), 0) == bags)
         for n in range(slots // 256):
             slot_hot = one_hot(lax.broadcasted_iota(jnp.int32, (256, LOOK_BLOCK), 0) + n * 256 == order)
@@ -149,8 +148,8 @@
 
 
 def cross_kernel(
-    cap, own_ref, count_hbm, rows_ref, weight_ref, bias_ref, up_ref, out_ref, grad_ref,
-    small_ref, count_ref, base_s, turned_s, sems,
+    cap, own_ref, low_hbm, high_hbm, rows_ref, weight_hbm, bias_ref, up_ref, out_ref, grad_ref,
+    small_ref, count_ref, weight_ref, base_s, turned_s, sems, weight_sem,
 ):
     cuts, owners, lanes = rows_ref.shape
     columns = lanes // cap
@@ -159,12 +158,17 @@
     own = own_ref[0]
     half = pairs * batch
     chunk = 4 * batch
+    width = low_hbm.shape[1]
     copies = []
-    for c in range(half // chunk):
-        for side in range(2):
-            part = pl.ds(side * half + c * chunk, chunk)
-            copies.append(pltpu.make_async_copy(count_hbm.at[part], small_ref.at[part], sems.at[2 * c + side]))
-            copies[-1].start()
+    for k in range(sems.shape[0]):
+        source = (low_hbm, high_hbm)[k % 2]
+        rows = source.shape[0] * 2 // sems.shape[0]
+        part = pl.ds(k // 2 * rows, rows)
+        copies.append(pltpu.make_async_copy(source.at[part], small_ref.at[k % 2, part], sems.at[k]))
+        copies[-1].start()
+
+    weight_copy = pltpu.make_async_copy(weight_hbm, weight_ref, weight_sem)
+    weight_copy.start()
 
     picked = swap_blocks([rows_ref[q].astype(jnp.float32) for q in range(cuts)], columns)
     rows = jnp.concatenate(picked, axis=0).astype(jnp.bfloat16)
@@ -180,11 +184,14 @@
 
     for copy in copies:
         copy.wait()
+    weight_copy.wait()
     for c in range(half // chunk):
         at = c * chunk
         for side in range(2):
             part = slice(side * half + at, side * half + at + chunk)
-            count_ref[part, :] = small_ref[part, :].astype(jnp.bfloat16)
+            for k in range(2):
+                cols = slice(k * width, (k + 1) * width)
+                count_ref[part, cols] = small_ref[k, part, :].astype(jnp.bfloat16)
         both = dot(count_ref[at : at + chunk, :], rows_even) + dot(
             count_ref[half + at : half + at + chunk, :], rows_odd
         )
@@ -267,18 +274,19 @@
     return call(scatter_kernel, jax.ShapeDtypeStruct((rows_out, LANES), jnp.float32), [V, V], limit=16, **kw)(ids, grads)
 
 
-def count(slot, bag, cap, tables, bags, slots, **kw):
+def count(slot, bag, cap, tables, bags, slots, side, **kw):
     V, S = pltpu.VMEM, pltpu.SMEM
-    out = jax.ShapeDtypeStruct((bags, slots), jnp.int8)
+    width = slots // 2
+    out = jax.ShapeDtypeStruct((bags, width), jnp.int8)
     pitch = tables + 1
     rows = (bags // tables - 1) * pitch + tables + window_rows(tables, pitch)
     rows = (rows + 7) // 8 * 8
     return call(
-        functools.partial(count_kernel, cap, tables, pitch),
+        functools.partial(count_kernel, cap, slots // cap, tables, pitch, side * width),
         out,
         [S, V, V],
         [
-            pltpu.VMEM((slots // LANES, rows, LANES), jnp.float32),
+            pltpu.VMEM((width // LANES, rows, LANES), jnp.float32),
             pltpu.VMEM(out.shape, out.dtype),
             pltpu.SemaphoreType.DMA((8,)),
         ],
@@ -288,25 +296,26 @@
     )(bag, slot, bag)
 
 
-def cross(own, counts, rows, weight, bias, up, cap, **kw):
+def cross(own, low, high, rows, weight, bias, up, cap, **kw):
     V, S = pltpu.VMEM, pltpu.SMEM
     cuts, owners, lanes = rows.shape
-    bags, slots = counts.shape
-    batch = up.shape[0]
+    bags, width = low.shape
     return call(
         functools.partial(cross_kernel, cap),
         (jax.ShapeDtypeStruct(up.shape, jnp.bfloat16), jax.ShapeDtypeStruct(rows.shape, jnp.bfloat16)),
-        [S, pltpu.HBM, V, V, V, V],
+        [S, pltpu.HBM, pltpu.HBM, V, pltpu.HBM, V, V],
         [
-            pltpu.VMEM(counts.shape, counts.dtype),
-            pltpu.VMEM(counts.shape, jnp.bfloat16),
+            pltpu.VMEM((2, bags, width), low.dtype),
+            pltpu.VMEM((bags, 2 * width), jnp.bfloat16),
+            pltpu.VMEM(weight.shape, weight.dtype),
             pltpu.VMEM((bags // 2, 2 * lanes), jnp.bfloat16),
             pltpu.VMEM((lanes, bags), jnp.bfloat16),
-            pltpu.SemaphoreType.DMA((bags // (4 * batch),)),
+            pltpu.SemaphoreType.DMA((8,)),
+            pltpu.SemaphoreType.DMA,
         ],
-        limit=48,
+        limit=50,
         **kw,
-    )(own, counts, rows, weight, bias, up)
+    )(own, low, high, rows, weight, bias, up)
 
 
 def per_device(embedding, cross_weight, cross_bias, upstream, unique_rows, lookup_slot, bag_of_lookup):
@@ -323,14 +332,17 @@
     picked = pick(ids, emb, owners, lanes)
     arrived = lax.all_to_all(picked, "table", 0, 0, tiled=True)
     sizes = (cap, tables, batch * tables, owners * cap)
-    counts = count(lookup_slot, bag_of_lookup, *sizes)
-    arrived, counts = lax.optimization_barrier((arrived, counts))
+    low = count(lookup_slot, bag_of_lookup, *sizes, 0)
+    arrived, low, lookup_slot, bag_of_lookup = lax.optimization_barrier(
+        (arrived, low, lookup_slot, bag_of_lookup)
+    )
     rows = lax.all_to_all(
         jnp.broadcast_to(arrived.reshape(1, owners, lanes), (cuts, owners, lanes)), "cuts", 0, 0, tiled=True
     )
+    high = count(lookup_slot, bag_of_lookup, *sizes, 1)
     own = lax.axis_index("cuts").astype(jnp.int32).reshape(1)
     cross_out, grads = cross(
-        own, counts, rows, cross_weight, cross_bias.reshape(1, share), upstream, cap
+        own, low, high, rows, cross_weight, cross_bias.reshape(1, share), upstream, cap
     )
     grads = lax.all_to_all(grads, "cuts", 0, 0, tiled=True)
     grads = jnp.sum(grads.astype(jnp.float32), axis=0).astype(jnp.bfloat16)

time: 125 us -> 122 us (0.976)
  blocking collectives: 45 us -> 42 us
  Pallas kernels: 20.5 us -> 22.7 us
  waiting for transfers between devices: 20.5 us -> 18.3 us
    all_to_all x1, waiting for transfers between devices: 7.32 us -> 1.75 us  [per_device(): lax.all_to_all(jnp.broadcast_to(arrived.reshape(1, owners, lanes), (cuts,...]
    all_to_all x1, blocking collectives: 34.2 us -> 29.8 us  [per_device(): returned = lax.all_to_all(grads, 'table', 0, 0, tiled=True)]
    all_to_all x1, waiting for transfers between devices: 13.2 us -> 16.6 us  [per_device(): arrived = lax.all_to_all(picked, 'table', 0, 0, tiled=True)]
    pallas_call x1 -> x2, Pallas kernels: 9.15 us -> 11.3 us  [count(): call(functools.partial(count_kernel, cap, slots // cap, tables, pitch, si...]
    all_to_all x1, blocking collectives: 10.8 us -> 12.2 us  [per_device(): grads = lax.all_to_all(grads, 'cuts', 0, 0, tiled=True)]
  transfers between devices with their start and end apart: 2 -> 2, of which waited for: 2 -> 2; matrix products, arithmetic and copies ran while one was open for 0% -> 0% of each run, Pallas kernels for 7% -> 9%
where the time goes in v5:
time: 122 us
  blocking collectives  42 us (34%)
  starting transfers between devices  37.2 us (30%)
  Pallas kernels  22.7 us (19%)
  waiting for transfers between devices  18.3 us (15%)
    all_to_all x1, starting transfers between devices, per_device(): arrived = lax.all_to_all(picked, 'table', 0, 0, tiled=True)  30.4 us
    all_to_all x1, blocking collectives, per_device(): returned = lax.all_to_all(grads, 'table', 0, 0, tiled=True)  29.8 us
    all_to_all x1, waiting for transfers between devices, per_device(): arrived = lax.all_to_all(picked, 'table', 0, 0, tiled=True)  16.6 us
    all_to_all x1, blocking collectives, per_device(): grads = lax.all_to_all(grads, 'cuts', 0, 0, tiled=True)  12.2 us
    pallas_call x2, Pallas kernels, count(): call(functools.partial(count_kernel, cap, slots // cap, tables, pitch, si...  11.3 us
    pallas_call x1, Pallas kernels, cross(): call(functools.partial(cross_kernel, cap), (jax.ShapeDtypeStruct(up.shape...  7.28 us
    all_to_all x1, starting transfers between devices, per_device(): lax.all_to_all(jnp.broadcast_to(arrived.reshape(1, owners, lanes), (cuts,...  6.75 us
    pallas_call x1, Pallas kernels, pick(): call(pick_kernel, out, [pltpu.HBM, pltpu.HBM], scratch, limit=62, **kw)  2.52 us
  transfers between devices with their start and end apart: 2, of which 2 were waited for; matrix products, arithmetic and copies ran while one was open for 0% of the time, Pallas kernels for 9%

profile of v5, /device:TPU:1, one launch (start us, length us, event | category | flops | bytes accessed | tf_op | source)
XLA Modules:
  0.0 121.8 jit_solution(7627043607636769364)
XLA Ops:
  0.6 2.5 %shard_map.86 = bf16[64,1,128]{2,1,0:T(2,128)(2,1)} custom-call(s32[16,64]{1,0:T(8,128)} %bitcast.27, bf16[1024,128]{1,0:T(8,128)(2,1)} %bitcast.31), custom_call_target="tpu_custom_call" | custom-call | tf_op jit(solution)/shard_map/pallas_call | solution.py:269
  3.2 30.4 %all-to-all-start = ((bf16[64,1,128]{2,1,0:T(2,128)(2,1)}), bf16[64,1,128]{2,1,0:T(2,128)(2,1)S(1)}, u32[]{:S(2)}, u32[]{:S(2)}) async-start(bf16[64,1,128]{2,1,0:T(2,128)(2,1)} %shard_map.86), calls=%async_computation | async-start | bytes 65536 | tf_op jit(solution)/shard_map/all_to_all | solution.py:333
  33.6 0.0 copy-start.1
  33.6 0.0 copy-start.3
  33.6 5.7 %shard_map.87.low_hbm = s8[4096,512]{1,0:T(32,128)(4,1)} custom-call(s32[1,8192]{1,0:T(1,128)} %bag_ref.2, s32[1,8192]{1,0:T(1,128)} %slot_ref.2, s32[1,8192]{1,0:T(1,128)} %bag_ref.2), custom_call_target="tpu_custom_call" | custom-call | tf_op jit(solution)/shard_map/pallas_call | solution.py:284
  39.3 0.0 copy-start
  39.4 16.6 %all-to-all-done = bf16[64,1,128]{2,1,0:T(2,128)(2,1)S(1)} async-done(((bf16[64,1,128]{2,1,0:T(2,128)(2,1)}), bf16[64,1,128]{2,1,0:T(2,128)(2,1)S(1)}, u32[]{:S(2)}, u32[]{:S(2)}) %all-to-all-start) | async-done | bytes 16416 | tf_op jit(solution)/shard_map/all_to_all | solution.py:333
  55.9 0.8 broadcast_in_dim.8
  56.7 6.8 %all-to-all-start.1 = ((bf16[16,64,128]{2,1,0:T(8,128)(2,1)}), bf16[16,64,128]{2,1,0:T(8,128)(2,1)S(1)}, u32[]{:S(2)}, u32[]{:S(2)}) async-start(bf16[16,64,128]{2,1,0:T(8,128)(2,1)} %broadcast_in_dim.8), calls=%async_computation.1 | async-start | bytes 524288 | tf_op jit(solution)/shard_map/all_to_all | solution.py:339
  63.5 5.6 %shard_map.88.high_hbm = s8[4096,512]{1,0:T(32,128)(4,1)} custom-call(s32[1,8192]{1,0:T(1,128)} %bag_ref.2, s32[1,8192]{1,0:T(1,128)} %slot_ref.2, s32[1,8192]{1,0:T(1,128)} %bag_ref.2), custom_call_target="tpu_custom_call" | custom-call | tf_op jit(solution)/shard_map/pallas_call | solution.py:284
  69.0 1.8 %all-to-all-done.1.rows_ref = bf16[16,64,128]{2,1,0:T(8,128)(2,1)S(1)} async-done(((bf16[16,64,128]{2,1,0:T(8,128)(2,1)}), bf16[16,64,128]{2,1,0:T(8,128)(2,1)S(1)}, u32[]{:S(2)}, u32[]{:S(2)}) %all-to-all-start.1) | async-done | bytes 262176 | tf_op jit(solution)/shard_map/all_to_all | solution.py:339
  70.8 0.0 copy-done.1
  70.8 0.0 copy-done.3
  70.8 0.0 copy-done
  70.8 0.0 copy-start.2
  70.8 7.3 %shard_map.89 = (bf16[128,256]{1,0:T(8,128)(2,1)}, bf16[16,64,128]{2,1,0:T(8,128)(2,1)S(1)}) custom-call(s32[1]{0:T(128)} %bitcast.own_ref, s8[4096,512]{1,0:T(32,128)(4,1)S(1)} %copy-done, s8[4096,512]{1,0:T(32,128)(4,1)} %shard_map.88.high_hbm, bf16[16,64,128]{2,1,0:T(8,128)(2,1)S(1)} %all-to-all-done.1.rows_ref, bf16[4096,256]{1,0:T(8,128)(2,1)} %weight_hbm.1, ...), custom_call_target="tpu_custom_call" | custom-call | tf_op jit(solution)/shard_map/pallas_call | solution.py:303
  78.1 12.2 %all_to_all.26 = bf16[16,64,128]{2,1,0:T(8,128)(2,1)S(1)} all-to-all(bf16[16,64,128]{2,1,0:T(8,128)(2,1)S(1)} %get-tuple-element.13), channel_id=1, replica_groups=mesh['table'=64,'cuts'=16] {'cuts'}, dimensions={0} | all-to-all | bytes 524288 | tf_op jit(solution)/shard_map/all_to_all | solution.py:347
  90.4 29.8 %all_to_all.27 = bf16[64,1,128]{2,1,0:T(2,128)(2,1)S(1)} all-to-all(bf16[64,1,128]{2,1,0:T(2,128)(2,1)S(1)} %copy.9), channel_id=1, replica_groups=mesh['table'=64,'cuts'=16] {'table'}, dimensions={0} | all-to-all | bytes 32768 | tf_op jit(solution)/shard_map/all_to_all | solution.py:349
  120.2 0.0 copy-done.2
  120.2 1.6 %shard_map.90 = f32[1024,128]{1,0:T(8,128)} custom-call(s32[16,64]{1,0:T(8,128)S(1)} %bitcast.28, bf16[64,128]{1,0:T(8,128)(2,1)S(1)} %bitcast.26), custom_call_target="tpu_custom_call" | custom-call | tf_op jit(solution)/shard_map/pallas_call | solution.py:274
  (4 shorter events, 0.1 us)
Async XLA Ops:
  3.2 52.8 %all-to-all-start = ((bf16[64,1,128]{2,1,0:T(2,128)(2,1)}), bf16[64,1,128]{2,1,0:T(2,128)(2,1)S(1)}, u32[]{:S(2)}, u32[]{:S(2)}) async-start(bf16[64,1,128]{2,1,0:T(2,128)(2,1)} %shard_map.86), calls=%async_computation | async-start | bytes 65536 | tf_op jit(solution)/shard_map/all_to_all | solution.py:333
  33.6 37.2 %copy-start.1 = (bf16[128,256]{1,0:T(8,128)(2,1)S(1)}, bf16[128,256]{1,0:T(8,128)(2,1)}, u32[]{:S(2)}) copy-start(bf16[128,256]{1,0:T(8,128)(2,1)} %up_ref.1) | copy-start | bytes 196612
  33.6 37.2 %copy-start.3 = (f32[256]{0:T(256)S(1)}, f32[256]{0:T(256)}, u32[]{:S(2)}) copy-start(f32[256]{0:T(256)} %param.9) | copy-start | bytes 3076
  39.3 31.4 %copy-start = (s8[4096,512]{1,0:T(32,128)(4,1)S(1)}, s8[4096,512]{1,0:T(32,128)(4,1)}, u32[]{:S(2)}) copy-start(s8[4096,512]{1,0:T(32,128)(4,1)} %shard_map.87.low_hbm) | copy-start | bytes 6291460
  56.7 14.1 %all-to-all-start.1 = ((bf16[16,64,128]{2,1,0:T(8,128)(2,1)}), bf16[16,64,128]{2,1,0:T(8,128)(2,1)S(1)}, u32[]{:S(2)}, u32[]{:S(2)}) async-start(bf16[16,64,128]{2,1,0:T(8,128)(2,1)} %broadcast_in_dim.8), calls=%async_computation.1 | async-start | bytes 524288 | tf_op jit(solution)/shard_map/all_to_all | solution.py:339
  70.8 49.4 %copy-start.2 = (s32[64,1,16]{0,2,1:T(8,128)S(1)}, s32[64,1,16]{0,2,1:T(8,128)}, u32[]{:S(2)}) copy-start(s32[64,1,16]{0,2,1:T(8,128)} %param.11) | copy-start | bytes 12292

commit v6 on v5

--- a/solution.py
+++ b/solution.py
@@ -60,16 +60,17 @@
     emb_copy.start()
     ids_copy.start()
     ids_copy.wait()
-    emb_copy.wait()
     cap, shards = ids_ref.shape
     columns = out_ref.shape[2] // cap
     highs = emb_ref.shape[0] // columns
-    per = 256 // shards
+    per = cap // 2
     pieces = []
     for group in range(cap // per):
         hi, lo = row_halves(ids_ref, group, per)
         n = hi.shape[1]
         low_hot = one_hot(lax.broadcasted_iota(jnp.int32, (LANES, n), 0) == lo)
+        if group == 0:
+            emb_copy.wait()
         wide = dot(emb_ref[...], low_hot).reshape(highs, columns, n)
         high_hot = lax.broadcasted_iota(jnp.int32, (highs, columns, n), 0) == hi[None]
         found = jnp.sum(jnp.where(high_hot, wide, 0.0), axis=0)
@@ -184,7 +185,6 @@
 
     for copy in copies:
         copy.wait()
-    weight_copy.wait()
     for c in range(half // chunk):
         at = c * chunk
         for side in range(2):
@@ -197,6 +197,7 @@
         )
         base_s[at : at + chunk, :] = both.astype(jnp.bfloat16)
 
+    weight_copy.wait()
     lane_block = lax.broadcasted_iota(jnp.int32, (batch, lanes), 1) // (2 * columns)
     per_half = lanes // (2 * columns)
     mix = jnp.zeros((batch, share), jnp.float32)

time: 122 us -> 122 us (level)
  no operation moved by 1% of the time
where the time goes in v6:
time: 122 us; the launch traced here: 121 us
  blocking collectives  42 us (34%)
  starting transfers between devices  37.2 us (30%)
  Pallas kernels  22 us (18%)
  waiting for transfers between devices  18.3 us (15%)
    all_to_all x1, starting transfers between devices, per_device(): arrived = lax.all_to_all(picked, 'table', 0, 0, tiled=True)  30.4 us
    all_to_all x1, blocking collectives, per_device(): returned = lax.all_to_all(grads, 'table', 0, 0, tiled=True)  29.8 us
    all_to_all x1, waiting for transfers between devices, per_device(): arrived = lax.all_to_all(picked, 'table', 0, 0, tiled=True)  16.6 us
    all_to_all x1, blocking collectives, per_device(): grads = lax.all_to_all(grads, 'cuts', 0, 0, tiled=True)  12.2 us
    pallas_call x2, Pallas kernels, count(): call(functools.partial(count_kernel, cap, slots // cap, tables, pitch, si...  11.3 us
    all_to_all x1, starting transfers between devices, per_device(): lax.all_to_all(jnp.broadcast_to(arrived.reshape(1, owners, lanes), (cuts,...  6.76 us
    pallas_call x1, Pallas kernels, cross(): call(functools.partial(cross_kernel, cap), (jax.ShapeDtypeStruct(up.shape...  6.65 us
  transfers between devices with their start and end apart: 2, of which 2 were waited for; matrix products, arithmetic and copies ran while one was open for 0% of the time, Pallas kernels for 9%

profile of v6, /device:TPU:1, one launch (start us, length us, event | category | flops | bytes accessed | tf_op | source)
XLA Modules:
  0.0 121.1 jit_solution(17577554058952621269)
XLA Ops:
  0.6 2.4 %shard_map.86 = bf16[64,1,128]{2,1,0:T(2,128)(2,1)} custom-call(s32[16,64]{1,0:T(8,128)} %bitcast.27, bf16[1024,128]{1,0:T(8,128)(2,1)} %bitcast.31), custom_call_target="tpu_custom_call" | custom-call | tf_op jit(solution)/shard_map/pallas_call | solution.py:270
  3.1 30.4 %all-to-all-start = ((bf16[64,1,128]{2,1,0:T(2,128)(2,1)}), bf16[64,1,128]{2,1,0:T(2,128)(2,1)S(1)}, u32[]{:S(2)}, u32[]{:S(2)}) async-start(bf16[64,1,128]{2,1,0:T(2,128)(2,1)} %shard_map.86), calls=%async_computation | async-start | bytes 65536 | tf_op jit(solution)/shard_map/all_to_all | solution.py:334
  33.5 0.0 copy-start.1
  33.5 0.0 copy-start.3
  33.5 5.7 %shard_map.87.low_hbm = s8[4096,512]{1,0:T(32,128)(4,1)} custom-call(s32[1,8192]{1,0:T(1,128)} %bag_ref.2, s32[1,8192]{1,0:T(1,128)} %slot_ref.2, s32[1,8192]{1,0:T(1,128)} %bag_ref.2), custom_call_target="tpu_custom_call" | custom-call | tf_op jit(solution)/shard_map/pallas_call | solution.py:285
  39.2 0.0 copy-start
  39.3 16.6 %all-to-all-done = bf16[64,1,128]{2,1,0:T(2,128)(2,1)S(1)} async-done(((bf16[64,1,128]{2,1,0:T(2,128)(2,1)}), bf16[64,1,128]{2,1,0:T(2,128)(2,1)S(1)}, u32[]{:S(2)}, u32[]{:S(2)}) %all-to-all-start) | async-done | bytes 16416 | tf_op jit(solution)/shard_map/all_to_all | solution.py:334
  55.8 0.8 broadcast_in_dim.8
  56.6 6.8 %all-to-all-start.1 = ((bf16[16,64,128]{2,1,0:T(8,128)(2,1)}), bf16[16,64,128]{2,1,0:T(8,128)(2,1)S(1)}, u32[]{:S(2)}, u32[]{:S(2)}) async-start(bf16[16,64,128]{2,1,0:T(8,128)(2,1)} %broadcast_in_dim.8), calls=%async_computation.1 | async-start | bytes 524288 | tf_op jit(solution)/shard_map/all_to_all | solution.py:340
  63.4 5.6 %shard_map.88.high_hbm = s8[4096,512]{1,0:T(32,128)(4,1)} custom-call(s32[1,8192]{1,0:T(1,128)} %bag_ref.2, s32[1,8192]{1,0:T(1,128)} %slot_ref.2, s32[1,8192]{1,0:T(1,128)} %bag_ref.2), custom_call_target="tpu_custom_call" | custom-call | tf_op jit(solution)/shard_map/pallas_call | solution.py:285
  68.9 1.8 %all-to-all-done.1.rows_ref = bf16[16,64,128]{2,1,0:T(8,128)(2,1)S(1)} async-done(((bf16[16,64,128]{2,1,0:T(8,128)(2,1)}), bf16[16,64,128]{2,1,0:T(8,128)(2,1)S(1)}, u32[]{:S(2)}, u32[]{:S(2)}) %all-to-all-start.1) | async-done | bytes 262176 | tf_op jit(solution)/shard_map/all_to_all | solution.py:340
  70.7 0.0 copy-done.1
  70.7 0.0 copy-done.3
  70.7 0.0 copy-done
  70.7 0.0 copy-start.2
  70.7 6.7 %shard_map.89 = (bf16[128,256]{1,0:T(8,128)(2,1)}, bf16[16,64,128]{2,1,0:T(8,128)(2,1)S(1)}) custom-call(s32[1]{0:T(128)} %bitcast.own_ref, s8[4096,512]{1,0:T(32,128)(4,1)S(1)} %copy-done, s8[4096,512]{1,0:T(32,128)(4,1)} %shard_map.88.high_hbm, bf16[16,64,128]{2,1,0:T(8,128)(2,1)S(1)} %all-to-all-done.1.rows_ref, bf16[4096,256]{1,0:T(8,128)(2,1)} %weight_hbm.1, ...), custom_call_target="tpu_custom_call" | custom-call | tf_op jit(solution)/shard_map/pallas_call | solution.py:304
  77.4 12.2 %all_to_all.26 = bf16[16,64,128]{2,1,0:T(8,128)(2,1)S(1)} all-to-all(bf16[16,64,128]{2,1,0:T(8,128)(2,1)S(1)} %get-tuple-element.13), channel_id=1, replica_groups=mesh['table'=64,'cuts'=16] {'cuts'}, dimensions={0} | all-to-all | bytes 524288 | tf_op jit(solution)/shard_map/all_to_all | solution.py:348
  89.6 29.8 %all_to_all.27 = bf16[64,1,128]{2,1,0:T(2,128)(2,1)S(1)} all-to-all(bf16[64,1,128]{2,1,0:T(2,128)(2,1)S(1)} %copy.9), channel_id=1, replica_groups=mesh['table'=64,'cuts'=16] {'table'}, dimensions={0} | all-to-all | bytes 32768 | tf_op jit(solution)/shard_map/all_to_all | solution.py:350
  119.5 0.0 copy-done.2
  119.5 1.6 %shard_map.90 = f32[1024,128]{1,0:T(8,128)} custom-call(s32[16,64]{1,0:T(8,128)S(1)} %bitcast.28, bf16[64,128]{1,0:T(8,128)(2,1)S(1)} %bitcast.26), custom_call_target="tpu_custom_call" | custom-call | tf_op jit(solution)/shard_map/pallas_call | solution.py:275
  (4 shorter events, 0.1 us)
Async XLA Ops:
  3.1 52.8 %all-to-all-start = ((bf16[64,1,128]{2,1,0:T(2,128)(2,1)}), bf16[64,1,128]{2,1,0:T(2,128)(2,1)S(1)}, u32[]{:S(2)}, u32[]{:S(2)}) async-start(bf16[64,1,128]{2,1,0:T(2,128)(2,1)} %shard_map.86), calls=%async_computation | async-start | bytes 65536 | tf_op jit(solution)/shard_map/all_to_all | solution.py:334
  33.5 37.2 %copy-start.1 = (bf16[128,256]{1,0:T(8,128)(2,1)S(1)}, bf16[128,256]{1,0:T(8,128)(2,1)}, u32[]{:S(2)}) copy-start(bf16[128,256]{1,0:T(8,128)(2,1)} %up_ref.1) | copy-start | bytes 196612
  33.5 37.2 %copy-start.3 = (f32[256]{0:T(256)S(1)}, f32[256]{0:T(256)}, u32[]{:S(2)}) copy-start(f32[256]{0:T(256)} %param.9) | copy-start | bytes 3076
  39.2 31.4 %copy-start = (s8[4096,512]{1,0:T(32,128)(4,1)S(1)}, s8[4096,512]{1,0:T(32,128)(4,1)}, u32[]{:S(2)}) copy-start(s8[4096,512]{1,0:T(32,128)(4,1)} %shard_map.87.low_hbm) | copy-start | bytes 6291460
  56.6 14.1 %all-to-all-start.1 = ((bf16[16,64,128]{2,1,0:T(8,128)(2,1)}), bf16[16,64,128]{2,1,0:T(8,128)(2,1)S(1)}, u32[]{:S(2)}, u32[]{:S(2)}) async-start(bf16[16,64,128]{2,1,0:T(8,128)(2,1)} %broadcast_in_dim.8), calls=%async_computation.1 | async-start | bytes 524288 | tf_op jit(solution)/shard_map/all_to_all | solution.py:340
  70.7 48.8 %copy-start.2 = (s32[64,1,16]{0,2,1:T(8,128)S(1)}, s32[64,1,16]{0,2,1:T(8,128)}, u32[]{:S(2)}) copy-start(s32[64,1,16]{0,2,1:T(8,128)} %param.11) | copy-start | bytes 12292
